TPU v7x, 256 devices: a whole 4x4x8 slice. The times are simulated.
256 devices in a mesh: dp: 16 (over y, x), ctx: 16 (over z, core).
Axes of the slice: x: 4, y: 4, z: 8, core: 2. Of those that a mesh axis runs over, the one named last changes fastest.
Arguments:
- queries: bfloat16 [32768, 12288], P(('dp', 'ctx')), may hold values from -8 to 8
- latent: bfloat16 [32768, 576], P(('dp', 'ctx')), may hold values from -8 to 8
- w_kv: bfloat16 [512, 16384], P(None, 'ctx'), may hold values from -0.25 to 0.25
- grad_out: bfloat16 [32768, 8192], P(('dp', 'ctx')), may hold values from -6 to 6
- doc_lengths: int32 [16, 16], replicated, may hold values from 1 to 256, 2048 in all within a row
- matching: int32 [16], replicated, may hold values from 0 to 15, each once
Outputs:
- grad_queries: bfloat16 [32768, 12288], P(('dp', 'ctx'))
- grad_latent: float32 [32768, 576], P(('dp', 'ctx'))
- grad_weight: float32 [512, 16384], P('dp', 'ctx')
Inputs may be any that keep to these rules, and one draw needn't show every extreme that they name: `doc_lengths`: each row sums to 2048, and its largest length is 256. `matching`: a permutation of the packs.
All inputs are finite; a program needn't handle non-finite values.
Results may differ from a plain program's by a relative error of at most 0.013.
Values may be sent and summed in bfloat16 or wider, within the bound.
A program may use at most 128 MiB of HBM per device.

v0:
```python
import jax
import jax.numpy as jnp
from jax import lax
from jax.sharding import PartitionSpec as P

NOPE = 128
ROPE = 64
VDIM = 128
LATENT = 512
QBLK = 256
MOST = 256


def windowed(values_in, count_of_blocks):
    split_rows = values_in.reshape(count_of_blocks, QBLK, values_in.shape[-1])
    earlier = jnp.concatenate([jnp.zeros_like(split_rows[:1]), split_rows[:-1]], axis=0)
    return jnp.concatenate([earlier, split_rows], axis=1)


def restore_from_span(window_grad, count_of_blocks, sequence_length):
    tail_part = window_grad[:, :MOST]
    own_part = window_grad[:, MOST:]
    padding = jnp.zeros((count_of_blocks, QBLK - MOST, window_grad.shape[-1]), jnp.float32)
    spilled = jnp.concatenate([padding, tail_part], axis=1)
    moved = jnp.concatenate([spilled[1:], jnp.zeros_like(spilled[:1])], axis=0)
    return (own_part + moved).reshape(sequence_length, window_grad.shape[-1])


def head_grads(query_rows, kv_rows, rope_rows, grad_rows, segment):
    sequence_length = query_rows.shape[0]
    count_of_blocks = sequence_length // QBLK
    logit_scale = float(NOPE + ROPE) ** (-0.5)
    key_rows = jnp.concatenate([kv_rows[:, :NOPE], rope_rows], axis=1)
    value_rows = kv_rows[:, NOPE:]
    blocked_queries = query_rows.reshape(count_of_blocks, QBLK, -1)
    key_span_rows = windowed(key_rows, count_of_blocks)
    value_span_rows = windowed(value_rows, count_of_blocks)
    block_gradients = grad_rows.reshape(count_of_blocks, QBLK, -1)
    seg_query = segment.reshape(count_of_blocks, QBLK)
    seg_key = windowed(segment[:, None], count_of_blocks)[:, :, 0]
    query_place = jnp.arange(sequence_length, dtype=jnp.int32).reshape(count_of_blocks, QBLK)
    key_place = query_place[:, :1] - MOST + jnp.arange(QBLK + MOST, dtype=jnp.int32)[None, :]
    allowed = (
        (key_place[:, None, :] >= 0)
        & (key_place[:, None, :] <= query_place[:, :, None])
        & (seg_key[:, None, :] == seg_query[:, :, None])
    )
    logit_matrix = (
        jnp.einsum(
            "roj,rmj->rom", blocked_queries, key_span_rows, preferred_element_type=jnp.float32
        )
        * logit_scale
    )
    logit_matrix = jnp.where(allowed, logit_matrix, -jnp.inf)
    attn_weights = jax.nn.softmax(logit_matrix, axis=-1)
    reduced_precision_weights = attn_weights.astype(jnp.bfloat16)
    attention_output = jnp.einsum(
        "yge,yel->ygl",
        reduced_precision_weights,
        value_span_rows,
        preferred_element_type=jnp.float32,
    )
    row_dot = jnp.sum(
        block_gradients.astype(jnp.float32) * attention_output, axis=-1, keepdims=True
    )
    probability_gradient = jnp.einsum(
        "roj,rmj->rom", block_gradients, value_span_rows, preferred_element_type=jnp.float32
    )
    score_gradient = (attn_weights * (probability_gradient - row_dot)).astype(jnp.bfloat16)
    query_gradient = (
        jnp.einsum(
            "yge,yel->ygl", score_gradient, key_span_rows, preferred_element_type=jnp.float32
        )
        * logit_scale
    )
    key_term = (
        jnp.einsum(
            "fle,flg->feg", score_gradient, blocked_queries, preferred_element_type=jnp.float32
        )
        * logit_scale
    )
    value_term = jnp.einsum(
        "fle,flg->feg",
        reduced_precision_weights,
        block_gradients,
        preferred_element_type=jnp.float32,
    )
    key_gradient = restore_from_span(key_term, count_of_blocks, sequence_length)
    value_gradient = restore_from_span(value_term, count_of_blocks, sequence_length)
    grad_kv_head = jnp.concatenate([key_gradient[:, :NOPE], value_gradient], axis=1)
    return (query_gradient.reshape(sequence_length, -1), grad_kv_head, key_gradient[:, NOPE:])


def body(queries, latent, w_kv, grad_out, doc_lengths, matching):
    groups = lax.axis_size("dp")
    row_total = queries.shape[0]
    piece_rows = row_total // groups
    width_qk = NOPE + ROPE
    width_kv = NOPE + VDIM
    group_index = lax.axis_index("dp")

    def split_rows(values_in):
        return values_in.reshape(groups, piece_rows, values_in.shape[1])

    def flatten_rows(values_in):
        return values_in.reshape(-1, values_in.shape[-1])

    source = matching[group_index]
    query_parts, latent_parts, grad_parts = (
        lax.all_to_all(split_rows(queries), "dp", split_axis=0, concat_axis=0, tiled=True),
        lax.all_to_all(split_rows(latent), "dp", split_axis=0, concat_axis=0, tiled=True),
        lax.all_to_all(split_rows(grad_out), "dp", split_axis=0, concat_axis=0, tiled=True),
    )
    query_parts = jnp.take(query_parts, matching, axis=0)
    latent_parts = jnp.take(latent_parts, matching, axis=0)
    grad_parts = jnp.take(grad_parts, matching, axis=0)
    query_parts, latent_parts, grad_parts = (
        lax.all_to_all(query_parts, "dp", split_axis=0, concat_axis=0, tiled=True),
        lax.all_to_all(latent_parts, "dp", split_axis=0, concat_axis=0, tiled=True),
        lax.all_to_all(grad_parts, "dp", split_axis=0, concat_axis=0, tiled=True),
    )
    query_heads, grad_heads = (
        lax.all_to_all(flatten_rows(query_parts), "ctx", split_axis=1, concat_axis=0, tiled=True),
        lax.all_to_all(flatten_rows(grad_parts), "ctx", split_axis=1, concat_axis=0, tiled=True),
    )
    latent_mine = flatten_rows(latent_parts)
    latent_whole = lax.all_gather(latent_mine, "ctx", axis=0, tiled=True)
    sequence_length = query_heads.shape[0]
    local_heads = query_heads.shape[1] // width_qk
    doc_ends = jnp.cumsum(doc_lengths[source])
    token_place = jnp.arange(sequence_length, dtype=jnp.int32)
    segment = jnp.sum((token_place[:, None] >= doc_ends[None, :]).astype(jnp.int32), axis=1)
    latent_nope = latent_whole[:, :LATENT]
    rope_rows = latent_whole[:, LATENT:]
    key_values = jnp.dot(latent_nope, w_kv, preferred_element_type=jnp.float32).astype(jnp.bfloat16)
    query_stack = query_heads.reshape(sequence_length, local_heads, width_qk).transpose(1, 0, 2)
    kv_stack = key_values.reshape(sequence_length, local_heads, width_kv).transpose(1, 0, 2)
    grad_stack = grad_heads.reshape(sequence_length, local_heads, VDIM).transpose(1, 0, 2)
    query_gradient, grad_kv_heads, grad_rope = lax.map(
        lambda pieces: head_grads(pieces[0], pieces[1], rope_rows, pieces[2], segment),
        (query_stack, kv_stack, grad_stack),
    )
    grad_query_all = (
        query_gradient.transpose(1, 0, 2)
        .reshape(sequence_length, local_heads * width_qk)
        .astype(jnp.bfloat16)
    )
    grad_kv = (
        grad_kv_heads.transpose(1, 0, 2)
        .reshape(sequence_length, local_heads * width_kv)
        .astype(jnp.bfloat16)
    )
    rope_total = jnp.sum(grad_rope, axis=0)
    grad_queries = lax.all_to_all(grad_query_all, "ctx", split_axis=0, concat_axis=1, tiled=True)
    nope_part = lax.dot_general(
        grad_kv, w_kv, (((1,), (1,)), ((), ())), preferred_element_type=jnp.float32
    )
    grad_latent = lax.psum_scatter(
        jnp.concatenate([nope_part, rope_total], axis=1), "ctx", scatter_dimension=0, tiled=True
    )
    grad_weight = lax.psum_scatter(
        lax.dot_general(
            latent_nope, grad_kv, (((0,), (0,)), ((), ())), preferred_element_type=jnp.float32
        ),
        "dp",
        scatter_dimension=0,
        tiled=True,
    )
    return (grad_queries, grad_latent, grad_weight)


def solution(mesh):
    in_specs = (
        P(("dp", "ctx"), None),
        P(("dp", "ctx"), None),
        P(None, "ctx"),
        P(("dp", "ctx"), None),
        P(),
        P(),
    )
    out_specs = (P(("dp", "ctx"), None), P(("dp", "ctx"), None), P("dp", "ctx"))
    return jax.shard_map(body, mesh=mesh, in_specs=in_specs, out_specs=out_specs, check_vma=False)
```

profile of v0, /device:TPU:1, one launch (start us, length us, event | category | flops | bytes accessed | tf_op | source)
XLA Modules:
  0.0 685.5 jit_solution(11567341820059701434)
XLA Ops:
  8.3 14.4 %all_to_all.78 = bf16[16,8,576]{2,1,0:T(8,128)(2,1)S(1)} all-to-all(bf16[16,8,576]{2,1,0:T(8,128)(2,1)S(1)} %bitcast.187), channel_id=1, replica_groups=mesh['dp'=16,'ctx'=16] {'dp'}, dimensions={0} | all-to-all | bytes 294912 | tf_op jit(solution)/shard_map/all_to_all | solution.py:111
  22.7 30.9 %all_to_all.79 = bf16[16,8,8192]{2,1,0:T(8,128)(2,1)S(1)} all-to-all(bf16[16,8,8192]{2,1,0:T(8,128)(2,1)} %bitcast.185), channel_id=1, replica_groups=mesh['dp'=16,'ctx'=16] {'dp'}, dimensions={0} | all-to-all | bytes 4194304 | tf_op jit(solution)/shard_map/all_to_all | solution.py:112
  53.6 4.6 all-to-all-start
  61.6 37.0 %all-to-all-done = bf16[16,8,12288]{2,1,0:T(8,128)(2,1)} async-done(((bf16[16,8,12288]{2,1,0:T(8,128)(2,1)}), bf16[16,8,12288]{2,1,0:T(8,128)(2,1)}, u32[]{:S(2)}, u32[]{:S(2)}) %all-to-all-start) | async-done | bytes 3145760 | tf_op jit(solution)/shard_map/all_to_all | solution.py:110
  98.6 6.4 all-to-all-start.4
  108.2 4.3 gather_fusion
  112.5 6.7 all-to-all-start.6
  119.1 3.9 broadcast_select_fusion
  123.1 23.4 %all-to-all-done.6 = bf16[16,8,8192]{2,1,0:T(8,128)(2,1)S(1)} async-done(((bf16[16,8,8192]{2,1,0:T(8,128)(2,1)}), bf16[16,8,8192]{2,1,0:T(8,128)(2,1)S(1)}, u32[]{:S(2)}, u32[]{:S(2)}) %all-to-all-start.6) | async-done | bytes 2097184 | tf_op jit(solution)/shard_map/all_to_all | solution.py:120
  146.5 6.5 all-to-all-start.1
  156.3 39.1 %all-to-all-done.1 = bf16[16,8,12288]{2,1,0:T(8,128)(2,1)} async-done(((bf16[16,8,12288]{2,1,0:T(8,128)(2,1)}), bf16[16,8,12288]{2,1,0:T(8,128)(2,1)}, u32[]{:S(2)}, u32[]{:S(2)}) %all-to-all-start.1) | async-done | bytes 3145760 | tf_op jit(solution)/shard_map/all_to_all | solution.py:118
  195.4 11.9 %all-to-all-start.7 = ((bf16[128,16,512]{2,0,1:T(8,128)(2,1)}), bf16[128,16,512]{2,0,1:T(8,128)(2,1)S(1)}, u32[]{:S(2)}, u32[]{:S(2)}) async-start(bf16[128,16,512]{2,0,1:T(8,128)(2,1)} %copy.94), calls=%async_computation.7 | async-start | bytes 4194304 | tf_op jit(solution)/shard_map/all_to_all | solution.py:124
  212.6 43.6 %all-to-all-done.7 = bf16[128,16,512]{2,0,1:T(8,128)(2,1)S(1)} async-done(((bf16[128,16,512]{2,0,1:T(8,128)(2,1)}), bf16[128,16,512]{2,0,1:T(8,128)(2,1)S(1)}, u32[]{:S(2)}, u32[]{:S(2)}) %all-to-all-start.7) | async-done | bytes 2097184 | tf_op jit(solution)/shard_map/all_to_all | solution.py:124
  256.2 5.0 all-to-all-start.2
  265.7 78.8 %all-gather.2.cloned.1.call-done = bf16[2048,576]{0,1:T(8,128)(2,1)} async-done(((bf16[128,576]{0,1:T(8,128)(2,1)}), bf16[2048,576]{0,1:T(8,128)(2,1)}) %all-gather.2.cloned.1.call-update) | async-done | bytes 2359312 | tf_op jit(solution)/shard_map/all_gather | solution.py:127
  346.2 6.0 convolution_convert_fusion
  357.4 5.1 copy.91
  362.5 5.8 reshape.205
  368.3 163.2 %while.17 = (s32[]{:T(128)}, bf16[4,2048,192]{1,2,0:T(8,128)(2,1)}, bf16[4,2048,256]{1,2,0:T(8,128)(2,1)}, f32[4,2048,64]{1,2,0:T(8,128)}, s32[2048]{0:T(1024)S(...) while((s32[]{:T(128)}, bf16[4,2048,192]{1,2,0:T(8,128)(2,1)}, ...), condition=%wide.wide.region_6.7_spmd, body=%wide.wide.region_2.0_spmd.sunk | while | flops 2052016640 | bytes 122705432 | solution.py:139
  379.5 5.3 fusion.129
  396.5 4.2 convolution_multiply_fusion.8
  420.3 5.3 fusion.129
  437.3 4.2 convolution_multiply_fusion.8
  461.1 5.3 fusion.129
  478.1 4.2 convolution_multiply_fusion.8
  501.9 5.3 fusion.129
  518.9 4.2 convolution_multiply_fusion.8
  531.5 6.6 fusion.42
  540.6 4.6 fusion.56
  551.5 79.2 %all_to_all.80 = bf16[16,128,768]{1,2,0:T(8,128)(2,1)} all-to-all(bf16[16,128,768]{1,2,0:T(8,128)(2,1)S(1)} %copy.97), channel_id=1, replica_groups=mesh['dp'=16,'ctx'=16] {'ctx'}, dimensions={0} | all-to-all | bytes 6291456 | tf_op jit(solution)/shard_map/all_to_all | solution.py:154
  630.7 4.6 copy.98
  635.3 43.7 %reduce-scatter.3.cloned.1.call-done = f32[128,576]{0,1:T(8,128)} async-done(((f32[2048,576]{0,1:T(8,128)}), f32[128,576]{0,1:T(8,128)}) %reduce-scatter.3.cloned.1.call-update) | async-done | bytes 294928 | tf_op jit(solution)/shard_map/reduce_scatter | solution.py:158
  (264 shorter events, 159.1 us)
Async XLA Ops:
  7.2 339.1 %copy-start = (bf16[512,1024]{1,0:T(8,128)(2,1)S(1)}, bf16[512,1024]{1,0:T(8,128)(2,1)}, u32[]{:S(2)}) copy-start(bf16[512,1024]{1,0:T(8,128)(2,1)} %param.10) | copy-start | bytes 3145732
  53.6 4.6 copy-start.12
  53.6 45.0 %all-to-all-start = ((bf16[16,8,12288]{2,1,0:T(8,128)(2,1)}), bf16[16,8,12288]{2,1,0:T(8,128)(2,1)}, u32[]{:S(2)}, u32[]{:S(2)}) async-start(bf16[16,8,12288]{2,1,0:T(8,128)(2,1)} %bitcast.183), calls=%async_computation | async-start | bytes 6291456 | tf_op jit(solution)/shard_map/all_to_all | solution.py:110
  98.6 13.9 %all-to-all-start.4 = ((bf16[16,8,576]{2,1,0:T(8,128)(2,1)}), bf16[16,8,576]{2,1,0:T(8,128)(2,1)S(1)}, u32[]{:S(2)}, u32[]{:S(2)}) async-start(bf16[16,8,576]{2,1,0:T(8,128)(2,1)} %broadcast_select_fusion.2), calls=%async_computation.4 | async-start | bytes 327680 | tf_op jit(solution)/shard_map/all_to_all | solution.py:119
  112.5 34.0 %all-to-all-start.6 = ((bf16[16,8,8192]{2,1,0:T(8,128)(2,1)}), bf16[16,8,8192]{2,1,0:T(8,128)(2,1)S(1)}, u32[]{:S(2)}, u32[]{:S(2)}) async-start(bf16[16,8,8192]{2,1,0:T(8,128)(2,1)} %broadcast_select_fusion.1), calls=%async_computation.6 | async-start | bytes 4194304 | tf_op jit(solution)/shard_map/all_to_all | solution.py:120
  146.5 48.9 %all-to-all-start.1 = ((bf16[16,8,12288]{2,1,0:T(8,128)(2,1)}), bf16[16,8,12288]{2,1,0:T(8,128)(2,1)}, u32[]{:S(2)}, u32[]{:S(2)}) async-start(bf16[16,8,12288]{2,1,0:T(8,128)(2,1)} %broadcast_select_fusion), calls=%async_computation.1 | async-start | bytes 6291456 | tf_op jit(solution)/shard_map/all_to_all | solution.py:118
  195.4 60.9 %all-to-all-start.7 = ((bf16[128,16,512]{2,0,1:T(8,128)(2,1)}), bf16[128,16,512]{2,0,1:T(8,128)(2,1)S(1)}, u32[]{:S(2)}, u32[]{:S(2)}) async-start(bf16[128,16,512]{2,0,1:T(8,128)(2,1)} %copy.94), calls=%async_computation.7 | async-start | bytes 4194304 | tf_op jit(solution)/shard_map/all_to_all | solution.py:124
  256.2 101.2 %all-to-all-start.2 = ((bf16[128,16,768]{2,0,1:T(8,128)(2,1)}), bf16[128,16,768]{2,0,1:T(8,128)(2,1)}, u32[]{:S(2)}, u32[]{:S(2)}) async-start(bf16[128,16,768]{2,0,1:T(8,128)(2,1)} %copy.90), calls=%async_computation.2 | async-start | bytes 6291456 | tf_op jit(solution)/shard_map/all_to_all | solution.py:123
  261.2 83.4 %all-gather.2.cloned.1.call-start = ((), (), s32[]{:S(2)}) async-start(), calls=%async_computation.11 | async-start | bytes 2506752 | tf_op jit(solution)/shard_map/all_gather | solution.py:127
  262.1 373.3 %reduce-scatter.5.cloned.1.call-start = ((), (), s32[]{:S(2)}) async-start(), calls=%async_computation.13 | async-start | bytes 2228224 | tf_op jit(solution)/shard_map/reduce_scatter | solution.py:161
  371.9 7.6 %copy-start.3 = (bf16[24,8,8,256]{3,2,1,0:T(8,128)(2,1)}, bf16[24,8,8,256]{3,2,1,0:T(8,128)(2,1)S(1)}, u32[]{:S(2)}) copy-start(bf16[24,8,8,256]{3,2,1,0:T(8,128)(2,1)S(1)} %copy.150) | copy-start | bytes 2359300 | tf_op jit(solution)/shard_map/while
  375.4 4.0 copy-start.6
  384.8 2.7 copy-start.5
  384.8 2.7 copy-start.8
  384.8 2.7 copy-start.9
  412.6 7.6 %copy-start.3 = (bf16[24,8,8,256]{3,2,1,0:T(8,128)(2,1)}, bf16[24,8,8,256]{3,2,1,0:T(8,128)(2,1)S(1)}, u32[]{:S(2)}) copy-start(bf16[24,8,8,256]{3,2,1,0:T(8,128)(2,1)S(1)} %copy.150) | copy-start | bytes 2359300 | tf_op jit(solution)/shard_map/while
  416.2 4.0 copy-start.6
  425.6 2.7 copy-start.5
  425.6 2.7 copy-start.8
  425.6 2.7 copy-start.9
  453.4 7.6 %copy-start.3 = (bf16[24,8,8,256]{3,2,1,0:T(8,128)(2,1)}, bf16[24,8,8,256]{3,2,1,0:T(8,128)(2,1)S(1)}, u32[]{:S(2)}) copy-start(bf16[24,8,8,256]{3,2,1,0:T(8,128)(2,1)S(1)} %copy.150) | copy-start | bytes 2359300 | tf_op jit(solution)/shard_map/while
  457.0 4.0 copy-start.6
  466.4 2.7 copy-start.5
  466.4 2.7 copy-start.8
  466.4 2.7 copy-start.9
  494.2 7.6 %copy-start.3 = (bf16[24,8,8,256]{3,2,1,0:T(8,128)(2,1)}, bf16[24,8,8,256]{3,2,1,0:T(8,128)(2,1)S(1)}, u32[]{:S(2)}) copy-start(bf16[24,8,8,256]{3,2,1,0:T(8,128)(2,1)S(1)} %copy.150) | copy-start | bytes 2359300 | tf_op jit(solution)/shard_map/while
  497.8 4.0 copy-start.6
  507.2 2.7 copy-start.5
  507.2 2.7 copy-start.8
  507.2 2.7 copy-start.9
  538.1 140.9 %reduce-scatter.3.cloned.1.call-start = ((), (), s32[]{:S(2)}) async-start(), calls=%async_computation.12 | async-start | bytes 5013504 | tf_op jit(solution)/shard_map/reduce_scatter | solution.py:158
  540.6 4.6 copy-start.11
  (17 other events, 24.8 us)
Sparse Core Ops, SparseCore 0:
  264.4 80.1 all-gather.1
  538.2 76.1 reduce-scatter.4
  617.8 61.1 reduce-scatter.2
where the time goes:
time: 691 us; the launch traced here: 686 us
  waiting for transfers between devices  266 us (38%)
  local copies, waits for them, and re-layouts  127 us (18%)
  blocking collectives  124 us (18%)
  matrix products  69 us (10%)
  other arithmetic  41.5 us (6%)
  starting transfers between devices  41.3 us (6%)
  between operations  15.9 us (2%)
    all_to_all x1, blocking collectives, body(): lax.all_to_all(grad_query_all, 'ctx', split_axis=0, concat_axis=1, tiled=...  79.2 us
    all_gather x1, waiting for transfers between devices, body(): latent_whole = lax.all_gather(latent_mine, 'ctx', axis=0, tiled=True)  78.8 us
    reduce_scatter x1, waiting for transfers between devices, body(): lax.psum_scatter(jnp.concatenate([nope_part, rope_total], axis=1), 'ctx',...  43.7 us
    all_to_all x1, waiting for transfers between devices, body(): lax.all_to_all(flatten_rows(grad_parts), 'ctx', split_axis=1, concat_axis...  43.6 us
    all_to_all x1, waiting for transfers between devices, body(): lax.all_to_all(query_parts, 'dp', split_axis=0, concat_axis=0, tiled=True)  39.1 us
    all_to_all x1, waiting for transfers between devices, body(): lax.all_to_all(split_rows(queries), 'dp', split_axis=0, concat_axis=0, ti...  37 us
    all_to_all x1, blocking collectives, body(): lax.all_to_all(split_rows(grad_out), 'dp', split_axis=0, concat_axis=0, t...  30.9 us
    all_to_all x1, waiting for transfers between devices, body(): lax.all_to_all(grad_parts, 'dp', split_axis=0, concat_axis=0, tiled=True)  23.4 us
  transfers between devices with their start and end apart: 9, of which 6 were waited for; matrix products, arithmetic and copies ran while one was open for 8% of the time, Pallas kernels for 0%

commit v1 on v0

v1 whole, which is shorter than its diff:
```python
import functools

import jax
import jax.numpy as jnp
from jax import lax
from jax.experimental import pallas as pl
from jax.experimental.pallas import tpu as pltpu
from jax.sharding import PartitionSpec as P

NOPE = 128
ROPE = 64
VDIM = 128
LATENT = 512
HEADS = 64
ROWS = 128
QK = NOPE + ROPE
KV = NOPE + VDIM
WIDE = LATENT + ROPE
MESH = pl.DeviceIdType.MESH
ANY = pl.BlockSpec(memory_space=pl.ANY)
BF = jnp.bfloat16
F32 = jnp.float32
LOW = -1e30


def place():
    dp, ctx = lax.axis_index("dp"), lax.axis_index("ctx")
    return dp // 4, lax.rem(dp, 4), ctx // 2, lax.rem(ctx, 2)


def pick(axis, on_x, on_y):
    return (1 - axis) * on_x + axis * on_y


def wrap(value, n):
    return lax.rem(value + n, n)


def line_dp(axis, position, y, x):
    return pick(axis, 4 * y + position, 4 * position + x)


class Sender:
    def __init__(self):
        self.sent = []
        self.due = []

    def remote(self, src, dst, send_sem, recv_sem, device):
        copy = pltpu.make_async_remote_copy(
            src_ref=src, dst_ref=dst, send_sem=send_sem, recv_sem=recv_sem,
            device_id=device, device_id_type=MESH,
        )
        copy.start()
        self.sent.append(copy)
        return copy

    def local(self, src, dst, sem):
        copy = pltpu.make_async_copy(src, dst, sem)
        copy.start()
        self.due.append(copy)

    def finish(self):
        for copy in self.due:
            copy.wait()
        for copy in self.sent:
            copy.wait_recv()
        for copy in self.sent:
            copy.wait_send()


def signal(device):
    pl.semaphore_signal(pltpu.get_barrier_semaphore(), inc=1, device_id=device, device_id_type=MESH)


def call(kernel, name, number, out_shape, semaphores):
    return pl.pallas_call(
        kernel,
        out_shape=out_shape,
        in_specs=None,
        out_specs=jax.tree.map(lambda _: ANY, out_shape),
        scratch_shapes=[pltpu.SemaphoreType.DMA(s) for s in semaphores],
        compiler_params=pltpu.CompilerParams(collective_id=number, has_side_effects=True),
        name=name,
    )


def gather_kernel(q, latent, w, g, q_out, g_out, lat_out, w_out, send, recv, w_send, w_recv, w_send2, w_recv2):
    y, x, z, core = place()
    dp = 4 * y + x
    mine = pick(core, x, y)
    other = pick(core, y, x)
    before, after = wrap(z - 1, 8), wrap(z + 1, 8)
    w_axis = z // 4
    w_match = (pick(w_axis, x, y) == lax.rem(z, 4)).astype(jnp.int32)
    w_other = pick(w_axis, y, x)
    same_core = (w_axis == core).astype(jnp.int32)
    w_chip = 4 * core + mine

    for e in range(2):
        half = lax.rem(core + e, 2)
        for d in range(4):
            source = line_dp(core, wrap(mine - d, 4), y, x)
            if d or e:
                signal((source, 2 * z + half))
            signal((source, 2 * before + half))
    for d in range(1, 4):
        signal((line_dp(1 - core, wrap(other - d, 4), y, x), 2 * z + core))
    for b in range(2):
        away = (w_chip != z) | (core != b)

        @pl.when(away)
        def _():
            signal((dp, 2 * w_chip + b))

    barrier = pltpu.get_barrier_semaphore()
    pl.semaphore_wait(barrier, 18 + w_match * (8 - same_core))

    moves = Sender()
    w_rows = w.at[pl.ds(pl.multiple_of(w_other * (LATENT // 4), LATENT // 4), LATENT // 4)]
    w_width = w.shape[1]

    def w_slot(quarter, b):
        return w_out.at[quarter, :, pl.ds(pl.multiple_of(b * w_width, w_width), w_width)]

    def w_copy(dz):
        target = (dp, 2 * lax.rem(z + dz, 8) + w_axis)
        return pltpu.make_async_remote_copy(
            src_ref=w_rows, dst_ref=w_slot(w_other, core), send_sem=w_send.at[dz], recv_sem=w_recv.at[core],
            device_id=target, device_id_type=MESH,
        )

    @pl.when(w_match == 1)
    def _():
        @pl.when(same_core == 1)
        def _():
            pltpu.make_async_copy(w_rows, w_slot(w_other, core), w_recv.at[core]).start()

        @pl.when(same_core == 0)
        def _():
            w_copy(0).start()

        for dz in (4, 1, 7, 2, 6, 3, 5):
            w_copy(dz).start()

    q_width = q.shape[1] // 8
    g_width = g.shape[1] // 8
    for e in range(2):
        axis = lax.rem(core + e, 2)
        spot = pick(axis, x, y)
        for d in range(4):
            target = line_dp(axis, lax.rem(spot + d, 4), y, x)
            k = 4 * e + d
            lat_own = lat_out.at[spot, 2 + core]
            if d == 0 and e == 0:
                moves.local(latent, lat_own, recv.at[2, k])
            else:
                moves.remote(latent, lat_own, send.at[2, k], recv.at[2, k], (target, 2 * z + axis))
            moves.remote(latent, lat_out.at[spot, core], send.at[3, k], recv.at[3, k], (target, 2 * after + axis))
    for d in (2, 1, 3, 0):
        for e in range(2):
            axis = lax.rem(core + e, 2)
            spot = pick(axis, x, y)
            there = lax.rem(spot + d, 4)
            target = (line_dp(axis, there, y, x), 2 * z + axis)
            k = 4 * e + d
            q_part = q.at[:, pl.ds(pl.multiple_of((4 * axis + there) * q_width, q_width), q_width)]
            g_part = g.at[:, pl.ds(pl.multiple_of((4 * axis + there) * g_width, g_width), g_width)]
            if d == 0 and e == 0:
                moves.local(q_part, q_out.at[spot, core], recv.at[0, k])
                moves.local(g_part, g_out.at[spot, core], recv.at[1, k])
            else:
                moves.remote(q_part, q_out.at[spot, core], send.at[0, k], recv.at[0, k], target)
                moves.remote(g_part, g_out.at[spot, core], send.at[1, k], recv.at[1, k], target)

    for b in range(2):
        slot = w_slot(other, b)
        pltpu.make_async_copy(slot, slot, w_recv.at[b]).wait()
    for d in range(1, 4):
        target = (line_dp(1 - core, lax.rem(other + d, 4), y, x), 2 * z + core)
        moves.remote(w_out.at[other], w_out.at[other], w_send2.at[d], w_recv2.at[d], target)
    moves.finish()

    @pl.when(w_match == 1)
    def _():
        @pl.when(same_core == 0)
        def _():
            w_copy(0).wait_send()

        for dz in range(1, 8):
            w_copy(dz).wait_send()


def gather(q, latent, w, g):
    rows = q.shape[0]
    shapes = [
        jax.ShapeDtypeStruct((4, 2, rows, q.shape[1] // 8), BF),
        jax.ShapeDtypeStruct((4, 2, rows, g.shape[1] // 8), BF),
        jax.ShapeDtypeStruct((4, 4, rows, latent.shape[1]), BF),
        jax.ShapeDtypeStruct((4, w.shape[0] // 4, 2 * w.shape[1]), BF),
    ]
    run = pl.pallas_call(
        gather_kernel,
        out_shape=shapes,
        in_specs=[ANY] * 4,
        out_specs=[ANY] * 4,
        scratch_shapes=[
            pltpu.SemaphoreType.DMA((4, 8)),
            pltpu.SemaphoreType.DMA((4, 8)),
            pltpu.SemaphoreType.DMA((8,)),
            pltpu.SemaphoreType.DMA((2,)),
            pltpu.SemaphoreType.DMA((4,)),
            pltpu.SemaphoreType.DMA((4,)),
        ],
        compiler_params=pltpu.CompilerParams(collective_id=0, has_side_effects=True),
        name="gather_inputs",
    )
    return run(q, latent, w, g)


def nt(a, b):
    return lax.dot_general(a, b, (((1,), (1,)), ((), ())), preferred_element_type=F32)


def tn(a, b):
    return lax.dot_general(a, b, (((0,), (0,)), ((), ())), preferred_element_type=F32)


def nn(a, b):
    return jnp.dot(a, b, preferred_element_type=F32)


def heads_kernel(lo, q, g, lat, w, gq, d_halo, d_own, dw, kv, gkv, p_t, ds_t, dw_sum, rope_sum):
    step = pl.program_id(0)
    rows = q.shape[2]
    block = 2 * rows
    window = 4 * rows
    scale = float(QK) ** -0.5
    pairs = gq.shape[1]
    part = 2 * KV

    @pl.when(step == 0)
    def _():
        p_t[...] = jnp.zeros_like(p_t)
        ds_t[...] = jnp.zeros_like(ds_t)
        dw_sum[...] = jnp.zeros_like(dw_sum)

    rope_sum[...] = jnp.zeros_like(rope_sum)
    nope = lat[0, :, :, :LATENT].reshape(window, LATENT)
    rope = lat[0, :, :, LATENT:].reshape(window, ROPE)
    lows = lo[0]
    key_at = lax.broadcasted_iota(jnp.int32, (3 * rows, rows), 0)
    query_at = lax.broadcasted_iota(jnp.int32, (3 * rows, rows), 1)

    def project(i, _):
        cols = pl.ds(pl.multiple_of(i * part, part), part)
        kv[:, cols] = nn(nope, w[:, cols]).astype(BF)
        return 0

    lax.fori_loop(0, pairs, project, 0)

    def pair(i, _):
        q_two = q[0, :, :, pl.ds(pl.multiple_of(i * 2 * QK, 2 * QK), 2 * QK)].reshape(block, 2 * QK)
        g_two = g[0, :, :, pl.ds(pl.multiple_of(i * 2 * VDIM, 2 * VDIM), 2 * VDIM)].reshape(block, 2 * VDIM)
        cols = pl.ds(pl.multiple_of(i * part, part), part)
        kv_two = kv[:, cols]
        dq_two, dkv_two = [], []
        for h in range(2):
            qh = q_two[:, h * QK:(h + 1) * QK]
            gh = g_two[:, h * VDIM:(h + 1) * VDIM]
            kh = jnp.concatenate([kv_two[:, h * KV:h * KV + NOPE], rope], axis=1)
            vh = kv_two[:, h * KV + NOPE:(h + 1) * KV]
            scores = nt(kh, qh)
            dprobs = nt(vh, gh)
            for s in range(2):
                keys = slice(rows * s, rows * s + 3 * rows)
                queries = slice(rows * s, rows * s + rows)
                low = lows[:, queries] - rows * s
                seen = (key_at >= low) & (key_at <= query_at + block)
                sc = jnp.where(seen, scores[keys, queries] * scale, LOW)
                top = jnp.max(sc, axis=0, keepdims=True)
                ex = jnp.exp(sc - top)
                probs = ex * (1.0 / jnp.sum(ex, axis=0, keepdims=True))
                probs_low = probs.astype(BF)
                dp = dprobs[keys, queries]
                row_dot = jnp.sum(probs_low.astype(F32) * dp, axis=0, keepdims=True)
                p_t[h, keys, queries] = probs_low
                ds_t[h, keys, queries] = (probs * (dp - row_dot)).astype(BF)
            ds = ds_t[h]
            dq_two.append((tn(ds, kh) * scale).astype(BF))
            dk = nn(ds, qh) * scale
            dv = nn(p_t[h], gh)
            rope_sum[...] += dk[:, NOPE:]
            dkv_two += [dk[:, :NOPE].astype(BF), dv.astype(BF)]
        gkv[:, cols] = jnp.concatenate(dkv_two, axis=1)
        gq[0, i] = jnp.concatenate(dq_two, axis=1).reshape(2, rows, 2 * QK)
        return 0

    lax.fori_loop(0, pairs, pair, 0)

    d_nope = nt(gkv[...], w[...]).astype(BF)
    d_rope = rope_sum[...].astype(BF)
    d_halo[0, :, :LATENT] = d_nope[:block]
    d_halo[0, :, LATENT:] = d_rope[:block]
    d_own[0, :, :LATENT] = d_nope[block:]
    d_own[0, :, LATENT:] = d_rope[block:]

    def weight(i, _):
        cols = pl.ds(pl.multiple_of(i * part, part), part)
        dw_sum[:, cols] += tn(nope, gkv[:, cols])
        return 0

    lax.fori_loop(0, pairs, weight, 0)

    @pl.when(step == pl.num_programs(0) - 1)
    def _():
        dw[...] = dw_sum[...].astype(BF).reshape(dw.shape)


def heads_grads(lo, q, g, lat, w):
    packs, _, rows, q_width = q.shape
    g_width = g.shape[3]
    block, window = 2 * rows, 4 * rows
    w_width = w.shape[1]
    pairs = q_width // (2 * QK)
    once = pl.BlockSpec((LATENT, w_width), lambda i: (0, 0))
    return pl.pallas_call(
        heads_kernel,
        grid=(packs,),
        in_specs=[
            pl.BlockSpec((1, 1, block), lambda i: (i, 0, 0)),
            pl.BlockSpec((1, 2, rows, q_width), lambda i: (i, 0, 0, 0)),
            pl.BlockSpec((1, 2, rows, g_width), lambda i: (i, 0, 0, 0)),
            pl.BlockSpec((1, 4, rows, WIDE), lambda i: (i, 0, 0, 0)),
            once,
        ],
        out_specs=[
            pl.BlockSpec((1, pairs, 2, rows, 2 * QK), lambda i: (i, 0, 0, 0, 0)),
            pl.BlockSpec((1, block, WIDE), lambda i: (i, 0, 0)),
            pl.BlockSpec((1, block, WIDE), lambda i: (i, 0, 0)),
            pl.BlockSpec((4, LATENT // 4, w_width), lambda i: (0, 0, 0)),
        ],
        out_shape=[
            jax.ShapeDtypeStruct((packs, pairs, 2, rows, 2 * QK), BF),
            jax.ShapeDtypeStruct((packs, block, WIDE), BF),
            jax.ShapeDtypeStruct((packs, block, WIDE), BF),
            jax.ShapeDtypeStruct((4, LATENT // 4, w_width), BF),
        ],
        scratch_shapes=[
            pltpu.VMEM((window, w_width), BF),
            pltpu.VMEM((window, w_width), BF),
            pltpu.VMEM((2, window, block), BF),
            pltpu.VMEM((2, window, block), BF),
            pltpu.VMEM((LATENT, w_width), F32),
            pltpu.VMEM((window, ROPE), F32),
        ],
        compiler_params=pltpu.CompilerParams(
            dimension_semantics=("arbitrary",), vmem_limit_bytes=50 * 1024 * 1024
        ),
        name="heads_grads",
    )(lo, q, g, lat, w)


def spread_kernel(gq, d_halo, d_own, dw, relay, d_lat, dw_parts, send, recv, send2, recv2):
    y, x, z, core = place()
    mine = pick(core, x, y)
    other = pick(core, y, x)
    before, after = wrap(z - 1, 8), wrap(z + 1, 8)

    for e in range(2):
        source_core = lax.rem(core + e, 2)
        axis = 1 - source_core
        spot = pick(axis, x, y)
        for d in range(4):
            if d or e:
                signal((line_dp(axis, wrap(spot - d, 4), y, x), 2 * z + source_core))
    for d in range(4):
        source = line_dp(core, wrap(mine - d, 4), y, x)
        if d:
            signal((source, 2 * z + core))
        signal((source, 2 * after + core))
    pl.semaphore_wait(pltpu.get_barrier_semaphore(), 14)

    moves = Sender()
    for d in (2, 1, 3, 0):
        there = lax.rem(other + d, 4)
        target = line_dp(1 - core, there, y, x)
        for e in range(2):
            half = lax.rem(core + e, 2)
            k = 4 * e + d
            src, dst = gq.at[:, there, half], relay.at[core, other]
            if d == 0 and e == 0:
                moves.local(src, dst, recv.at[k])
            else:
                moves.remote(src, dst, send.at[k], recv.at[k], (target, 2 * z + half))
        if d == 0:
            moves.local(dw.at[there], dw_parts.at[other], recv2.at[0, d])
        else:
            moves.remote(dw.at[there], dw_parts.at[other], send2.at[0, d], recv2.at[0, d], (target, 2 * z + core))
        there = lax.rem(mine + d, 4)
        target = line_dp(core, there, y, x)
        if d == 0:
            moves.local(d_own.at[there], d_lat.at[0, mine], recv2.at[1, d])
        else:
            moves.remote(d_own.at[there], d_lat.at[0, mine], send2.at[1, d], recv2.at[1, d], (target, 2 * z + core))
        moves.remote(d_halo.at[there], d_lat.at[1, mine], send2.at[2, d], recv2.at[2, d], (target, 2 * before + core))
    moves.finish()


def spread(gq, d_halo, d_own, dw):
    packs, pairs, _, rows, width = gq.shape
    return pl.pallas_call(
        spread_kernel,
        out_shape=[
            jax.ShapeDtypeStruct((2, 4, packs, rows, width), BF),
            jax.ShapeDtypeStruct((2, 4) + d_own.shape[1:], BF),
            jax.ShapeDtypeStruct(dw.shape, BF),
        ],
        in_specs=[ANY] * 4,
        out_specs=[ANY] * 3,
        scratch_shapes=[
            pltpu.SemaphoreType.DMA((8,)),
            pltpu.SemaphoreType.DMA((8,)),
            pltpu.SemaphoreType.DMA((3, 4)),
            pltpu.SemaphoreType.DMA((3, 4)),
        ],
        compiler_params=pltpu.CompilerParams(collective_id=1, has_side_effects=True),
        name="spread_results",
    )(gq, d_halo, d_own, dw)


def deliver_kernel(chosen, d_lat, dw, gq, lat_relay, dw_parts, send, recv, send2, recv2, send3, recv3):
    y, x, z, core = place()
    dp = 4 * y + x
    ctx = 2 * z + core
    for d in range(16):
        there = lax.rem(dp + d, 16)
        if d:
            signal((there, ctx))
        signal((there, 2 * z + 1 - core))
    for d in range(1, 8):
        signal((dp, 2 * lax.rem(z + d, 8) + core))
    pl.semaphore_wait(pltpu.get_barrier_semaphore(), 38)

    moves = Sender()
    width = chosen.shape[3]
    for d in range(16):
        there = lax.rem(dp + d, 16)
        for e in range(2):
            half = lax.rem(core + e, 2)
            src, dst = d_lat.at[half, there], lat_relay.at[dp, core]
            if d == 0 and e == 0:
                moves.local(src, dst, recv2.at[e, d])
            else:
                moves.remote(src, dst, send2.at[e, d], recv2.at[e, d], (there, 2 * z + half))
    for d in range(16):
        there = lax.rem(dp + d, 16)
        for j, at in ((0, 4 * x + y), (1, 16 + 4 * y + x)):
            dst = gq.at[:, pl.ds(pl.multiple_of(at * width, width), width)]
            if d == 0:
                moves.local(chosen.at[there, j], dst, recv.at[j, d])
            else:
                moves.remote(chosen.at[there, j], dst, send.at[j, d], recv.at[j, d], (there, ctx))
    for d in range(8):
        there = lax.rem(z + d, 8)
        if d == 0:
            moves.local(dw.at[there], dw_parts.at[z], recv3.at[d])
        else:
            moves.remote(dw.at[there], dw_parts.at[z], send3.at[d], recv3.at[d], (dp, 2 * there + core))
    moves.finish()


def deliver(chosen, d_lat, dw):
    _, _, rows, width = chosen.shape
    return pl.pallas_call(
        deliver_kernel,
        out_shape=[
            jax.ShapeDtypeStruct((rows, 32 * width), BF),
            jax.ShapeDtypeStruct((16, 2) + d_lat.shape[2:], F32),
            jax.ShapeDtypeStruct(dw.shape, F32),
        ],
        in_specs=[ANY] * 3,
        out_specs=[ANY] * 3,
        scratch_shapes=[
            pltpu.SemaphoreType.DMA((2, 16)),
            pltpu.SemaphoreType.DMA((2, 16)),
            pltpu.SemaphoreType.DMA((2, 16)),
            pltpu.SemaphoreType.DMA((2, 16)),
            pltpu.SemaphoreType.DMA((8,)),
            pltpu.SemaphoreType.DMA((8,)),
        ],
        compiler_params=pltpu.CompilerParams(collective_id=2, has_side_effects=True),
        name="deliver_queries",
    )(chosen, d_lat, dw)


def weight_home(k):
    pairs = []
    for dp in range(16):
        for ctx in range(16):
            y, x, z, core = dp // 4, dp % 4, ctx // 2, ctx % 2
            mine, other = (x, y) if core == 0 else (y, x)
            piece = k ^ (z % 2)
            home = (4 * other + z // 2) * 16 + 8 * core + 2 * mine + piece
            pairs.append((dp * 16 + ctx, home))
    return pairs


def body(queries, latent, w_kv, grad_out, doc_lengths, matching):
    y, x, z, core = place()
    dp = 4 * y + x
    rows = queries.shape[0]
    block = 2 * rows

    packs = pick(core, 4 * y + jnp.arange(4), 4 * jnp.arange(4) + x)
    ends = jnp.cumsum(doc_lengths[packs], axis=1)
    token = z * block + jnp.arange(block, dtype=jnp.int32)
    begun = jnp.where(ends[:, None, :] <= token[None, :, None], ends[:, None, :], 0)
    lo = (jnp.max(begun, axis=2) - (z - 1) * block)[:, None, :].astype(jnp.int32)

    q_all, g_all, lat_all, w_all = gather(queries, latent, w_kv, grad_out)
    w_all = w_all.reshape(LATENT, w_all.shape[2])
    gq, d_halo, d_own, dw = heads_grads(lo, q_all, g_all, lat_all, w_all)
    relay, d_lat, dw_parts = spread(gq, d_halo, d_own, dw)

    major, minor = matching // 4, lax.rem(matching, 4)
    chosen = jnp.stack([relay[0][major, minor], relay[1][minor, major]], axis=1)
    d_lat = jnp.sum(d_lat.astype(F32), axis=(0, 1)).reshape(2, 16, rows // 16, WIDE)
    dw_mine = jnp.sum(dw_parts.astype(F32), axis=0)
    dw_mine = dw_mine.reshape(8, LATENT // 32, dw_mine.shape[1])
    grad_queries, lat_relay, dw_z = deliver(chosen, d_lat, dw_mine)

    lat_chosen = jnp.sum(lat_relay, axis=1)[matching]
    grad_latent = lax.all_to_all(lat_chosen, "dp", split_axis=0, concat_axis=0, tiled=True).reshape(rows, WIDE)

    dw_last = jnp.sum(dw_z, axis=0).reshape(LATENT // 32, 2, -1)
    odd = lax.rem(z, 2)
    arrived = [
        lax.ppermute(jnp.where(odd == k, dw_last[:, 0], dw_last[:, 1]), ("dp", "ctx"), weight_home(k))
        for k in range(2)
    ]
    grad_weight = jnp.concatenate(
        [jnp.where(core == 0, arrived[0], arrived[1]), jnp.where(core == 0, arrived[1], arrived[0])], axis=0
    )
    return grad_queries, grad_latent, grad_weight


def solution(mesh):
    in_specs = (
        P(("dp", "ctx"), None),
        P(("dp", "ctx"), None),
        P(None, "ctx"),
        P(("dp", "ctx"), None),
        P(),
        P(),
    )
    out_specs = (P(("dp", "ctx"), None), P(("dp", "ctx"), None), P("dp", "ctx"))
    return jax.shard_map(body, mesh=mesh, in_specs=in_specs, out_specs=out_specs, check_vma=False)
```

time: 691 us -> 284 us (0.41)
  waiting for transfers between devices: 266 us -> 7.43 us
  Pallas kernels: 0 us -> 234 us
  blocking collectives: 124 us -> 0 us
  local copies, waits for them, and re-layouts: 127 us -> 16.6 us
  matrix products: 69 us -> 0 us
  other arithmetic: 41.5 us -> 10.5 us
  starting transfers between devices: 41.3 us -> 14.2 us
  between operations: 15.9 us -> 0.87 us
    pallas_call x0 -> x4, Pallas kernels: none -> 234 us  [the longest x1 65.3 us: gather(): return run(q, latent, w, g)]
    all_to_all x6 -> x1, waiting for transfers between devices: 143 us -> 7.42 us  [body(): lax.all_to_all(lat_chosen, 'dp', split_axis=0, concat_axis=0, tiled=True)]
    all_to_all x3 -> x0, blocking collectives: 124 us -> none  [the longest x1 79.2 us: body(): lax.all_to_all(grad_query_all, 'ctx', split_axis=0, concat_axis=1, tiled=...]
    all_gather x1 -> x0, waiting for transfers between devices: 78.8 us -> none  [body(): latent_whole = lax.all_gather(latent_mine, 'ctx', axis=0, tiled=True)]
    dot_general x23 -> x0, matrix products: 47.9 us -> none  [the longest x4 16.6 us: head_grads(): jnp.einsum('fle,flg->feg', score_gradient, blocked_queries, preferred_ele...]
    reduce_scatter x2 -> x0, waiting for transfers between devices: 43.7 us -> none  [the longest x1 43.7 us: body(): lax.psum_scatter(jnp.concatenate([nope_part, rope_total], axis=1), 'ctx',...]
    all_to_all x6 -> x1, starting transfers between devices: 41 us -> 7.83 us  [body(): lax.all_to_all(lat_chosen, 'dp', split_axis=0, concat_axis=0, tiled=True)]
    slice x37 -> x0, local copies, waits for them, and re-layouts: 27.5 us -> none  [the longest x8 11.9 us: head_grads(): value_rows = kv_rows[:, NOPE:]]
  transfers between devices with their start and end apart: 9 -> 3, of which waited for: 6 -> 1; matrix products, arithmetic and copies ran while one was open for 8% -> 2% of each run, Pallas kernels for 0% -> 0%
where the time goes in v1:
time: 284 us; the launch traced here: 283 us
  Pallas kernels  234 us (82%)
  local copies, waits for them, and re-layouts  16.6 us (6%)
  starting transfers between devices  14.2 us (5%)
  other arithmetic  10.5 us (4%)
  waiting for transfers between devices  7.43 us (3%)
    pallas_call x1, Pallas kernels, gather(): return run(q, latent, w, g)  65.3 us
    pallas_call x1, Pallas kernels, deliver(): pl.pallas_call(deliver_kernel, out_shape=[jax.ShapeDtypeStruct((rows, 32...  61.2 us
    pallas_call x1, Pallas kernels, spread(): pl.pallas_call(spread_kernel, out_shape=[jax.ShapeDtypeStruct((2, 4, pack...  55.8 us
    pallas_call x1, Pallas kernels, heads_grads(): pl.pallas_call(heads_kernel, grid=(packs,), in_specs=[pl.BlockSpec((1, 1,...  51.2 us
    unnamed x20, local copies, waits for them, and re-layouts  8.39 us
    all_to_all x1, starting transfers between devices, body(): lax.all_to_all(lat_chosen, 'dp', split_axis=0, concat_axis=0, tiled=True)  7.83 us
    all_to_all x1, waiting for transfers between devices, body(): lax.all_to_all(lat_chosen, 'dp', split_axis=0, concat_axis=0, tiled=True)  7.42 us
    ppermute x2, starting transfers between devices, body(): lax.ppermute(jnp.where(odd == k, dw_last[:, 0], dw_last[:, 1]), ('dp', 'c...  6.41 us
  transfers between devices with their start and end apart: 3, of which 1 were waited for; matrix products, arithmetic and copies ran while one was open for 2% of the time, Pallas kernels for 0%

profile of v1, /device:TPU:1, one launch (start us, length us, event | category | flops | bytes accessed | tf_op | source)
XLA Modules:
  0.0 283.3 jit_solution(11565381113471475063)
XLA Ops:
  0.7 0.6 copy-done
  1.3 0.6 gather_fusion
  1.9 0.2 reduce_window_sum.11
  2.1 0.1 select_reduce_fusion
  2.2 1.7 copy.15.latent
  3.9 65.3 %gather_inputs.1 = (bf16[4,2,128,1536]{3,2,1,0:T(8,128)(2,1)}, bf16[4,2,128,1024]{3,2,1,0:T(8,128)(2,1)}, bf16[4,4,128,576]{3,2,1,0:T(8,128)(2,1)}, bf16[4,128,2048]{2,1,0:T(8,128)(2,1)}) custom-call(bf16[128,12288]{1,0:T(8,128)(2,1)} %q.1, bf16[128,576]{1,0:T(8,128)(2,1)} %copy.15.latent, bf16[512,1024]{1,0:T(8,128)(2,1)} %w.1, bf16[128,8192]{1,0:T(8,128)(2,1)} %g.1), custom_call_target="tpu_custom_call" | custom-call | tf_op jit(solution)/shard_map/gather_inputs/pallas_call | solution.py:217
  69.3 51.2 %heads_grads.1 = (bf16[4,4,2,128,384]{4,3,2,1,0:T(8,128)(2,1)}, bf16[4,256,576]{2,1,0:T(8,128)(2,1)S(1)}, bf16[4,256,576]{2,1,0:T(8,128)(2,1)S(1)}, bf16[4,128,2048]{2,1,0:T(8,128)(2,1)}) custom-call(s32[4,1,256]{2,1,0:T(1,128)S(1)} %sub.39.lo, bf16[4,2,128,1536]{3,2,1,0:T(8,128)(2,1)} %get-tuple-element.17.q, ...), custom_call_target="tpu_custom_call" | custom-call | tf_op jit(solution)/shard_map/heads_grads/pallas_call | solution.py:326
  120.5 1.1 copy-done.1
  121.5 1.0 copy-done.2
  122.6 55.8 %spread_results.1 = (bf16[2,4,4,128,384]{4,3,2,1,0:T(8,128)(2,1)}, bf16[2,4,256,576]{3,2,1,0:T(8,128)(2,1)}, bf16[4,128,2048]{2,1,0:T(8,128)(2,1)}) custom-call(bf16[4,4,2,128,384]{4,3,2,1,0:T(8,128)(2,1)} %get-tuple-element.21.gq, bf16[4,256,576]{2,1,0:T(8,128)(2,1)} %copy-done.1, bf16[4,256,576]{2,1,0:T(8,128)(2,1)} %copy-done.2, ...), custom_call_target="tpu_custom_call" | custom-call | tf_op jit(solution)/shard_map/spread_results/pallas_call | solution.py:411
  178.4 2.4 slice_bitcast_fusion.1
  180.9 0.1 copy-done.6
  181.0 1.4 convert_reduce_fusion.1
  182.4 0.6 copy-done.5
  183.0 1.2 convert_reduce_fusion
  184.2 1.9 gather_fusion.2
  186.2 1.9 gather_fusion.1
  188.1 3.4 %pad_maximum_fusion.chosen = bf16[16,2,128,384]{3,2,1,0:T(8,128)(2,1)} fusion(bf16[16,1,128,384]{3,2,1,0:T(8,128)(2,1)S(1)} %bitcast.17, bf16[16,1,128,384]{3,2,1,0:T(8,128)(2,1)} %bitcast.18), kind=kLoop, calls=%fused_computation.6 | loop fusion | flops 1572864 | bytes 6291456 | tf_op jit(solution)/shard_map/stack | solution.py:526
  191.5 61.2 %deliver_queries.1 = (bf16[128,12288]{1,0:T(8,128)(2,1)}, f32[16,2,8,576]{3,2,1,0:T(8,128)}, f32[8,16,2048]{2,1,0:T(8,128)}) custom-call(bf16[16,2,128,384]{3,2,1,0:T(8,128)(2,1)} %pad_maximum_fusion.chosen, f32[2,16,8,576]{3,2,1,0:T(8,128)} %bitcast.20, f32[8,16,2048]{2,1,0:T(8,128)} %bitcast.19), custom_call_target="tpu_custom_call" | custom-call | tf_op jit(solution)/shard_map/deliver_queries/pallas_call | solution.py:474
  252.8 1.3 reduce_sum.39
  254.1 0.1 reshape.80
  254.2 0.1 fusion.5
  254.3 6.4 %collective-permute-start = (f32[16,1024]{1,0:T(8,128)S(1)}, f32[16,1024]{1,0:T(8,128)}, u32[]{:S(2)}, u32[]{:S(2)}) collective-permute-start(f32[16,1024]{1,0:T(8,128)S(1)} %fusion), channel_id=1, source_target_pairs={{0,0},{1,8},{2,1},{3,9},{4,16},{5,24},{6,17},{7,25},{8,32},{9,40},... | collective-permute-start | bytes 196616 | tf_op jit(solution)/shard_map/ppermute | solution.py:538
  260.8 0.6 copy.27
  261.4 1.2 reduce_sum.38
  262.6 1.3 gather_fusion.3
  263.9 7.8 %all-to-all-start = ((f32[16,8,576]{2,1,0:T(8,128)}), f32[16,8,576]{2,1,0:T(8,128)S(1)}, u32[]{:S(2)}, u32[]{:S(2)}) async-start(f32[16,8,576]{2,1,0:T(8,128)} %gather_fusion.3), calls=%async_computation | async-start | bytes 655360 | tf_op jit(solution)/shard_map/all_to_all | solution.py:533
  271.7 0.9 broadcast_select_fusion.2
  272.6 0.7 pad_maximum_fusion.1
  273.3 7.4 %all-to-all-done = f32[16,8,576]{2,1,0:T(8,128)S(1)} async-done(((f32[16,8,576]{2,1,0:T(8,128)}), f32[16,8,576]{2,1,0:T(8,128)S(1)}, u32[]{:S(2)}, u32[]{:S(2)}) %all-to-all-start) | async-done | bytes 294944 | tf_op jit(solution)/shard_map/all_to_all | solution.py:533
  280.7 0.9 copy.19
  281.6 1.7 copy.29
  (23 shorter events, 0.1 us)
Async XLA Ops:
  0.6 0.7 copy-start
  120.5 1.1 copy-start.1
  121.5 1.1 copy-start.2
  178.4 2.4 copy-start.7
  178.4 2.5 copy-start.6
  180.8 2.2 copy-start.5
  186.2 1.9 copy-start.3
  254.2 27.4 %copy-start.4 = (bf16[128,12288]{1,0:T(8,128)(2,1)S(1)}, bf16[128,12288]{1,0:T(8,128)(2,1)}, u32[]{:S(2)}) copy-start(bf16[128,12288]{1,0:T(8,128)(2,1)} %get-tuple-element.51) | copy-start | bytes 9437188
  254.3 17.4 %collective-permute-start = (f32[16,1024]{1,0:T(8,128)S(1)}, f32[16,1024]{1,0:T(8,128)}, u32[]{:S(2)}, u32[]{:S(2)}) collective-permute-start(f32[16,1024]{1,0:T(8,128)S(1)} %fusion), channel_id=1, source_target_pairs={{0,0},{1,8},{2,1},{3,9},{4,16},{5,24},{6,17},{7,25},{8,32},{9,40},... | collective-permute-start | bytes 196616 | tf_op jit(solution)/shard_map/ppermute | solution.py:538
  261.4 10.3 %collective-permute-start.1 = (f32[16,1024]{1,0:T(8,128)}, f32[16,1024]{1,0:T(8,128)}, u32[]{:S(2)}, u32[]{:S(2)}) collective-permute-start(f32[16,1024]{1,0:T(8,128)} %bitcast.16), channel_id=1, source_target_pairs={{0,1},{1,9},{2,0},{3,8},{4,17},{5,25},{6,16},{7,24},{8,33},{9,41},... | collective-permute-start | bytes 196616 | tf_op jit(solution)/shard_map/ppermute | solution.py:538
  263.9 16.8 %all-to-all-start = ((f32[16,8,576]{2,1,0:T(8,128)}), f32[16,8,576]{2,1,0:T(8,128)S(1)}, u32[]{:S(2)}, u32[]{:S(2)}) async-start(f32[16,8,576]{2,1,0:T(8,128)} %gather_fusion.3), calls=%async_computation | async-start | bytes 655360 | tf_op jit(solution)/shard_map/all_to_all | solution.py:533

commit v2 on v1

v2 whole, which is shorter than its diff:
```python
import functools

import jax
import jax.numpy as jnp
from jax import lax
from jax.experimental import pallas as pl
from jax.experimental.pallas import tpu as pltpu
from jax.sharding import PartitionSpec as P

NOPE = 128
ROPE = 64
VDIM = 128
LATENT = 512
HEADS = 64
ROWS = 128
QK = NOPE + ROPE
KV = NOPE + VDIM
WIDE = LATENT + ROPE
MESH = pl.DeviceIdType.MESH
ANY = pl.BlockSpec(memory_space=pl.ANY)
BF = jnp.bfloat16
F32 = jnp.float32
LOW = -1e30


def place():
    dp, ctx = lax.axis_index("dp"), lax.axis_index("ctx")
    return dp // 4, lax.rem(dp, 4), ctx // 2, lax.rem(ctx, 2)


def pick(axis, on_x, on_y):
    return (1 - axis) * on_x + axis * on_y


def wrap(value, n):
    return lax.rem(value + n, n)


def line_dp(axis, position, y, x):
    return pick(axis, 4 * y + position, 4 * position + x)


class Sender:
    def __init__(self):
        self.sent = []
        self.due = []

    def remote(self, src, dst, send_sem, recv_sem, device):
        copy = pltpu.make_async_remote_copy(
            src_ref=src, dst_ref=dst, send_sem=send_sem, recv_sem=recv_sem,
            device_id=device, device_id_type=MESH,
        )
        copy.start()
        self.sent.append(copy)
        return copy

    def local(self, src, dst, sem):
        copy = pltpu.make_async_copy(src, dst, sem)
        copy.start()
        self.due.append(copy)

    def finish(self):
        for copy in self.due:
            copy.wait()
        for copy in self.sent:
            copy.wait_recv()
        for copy in self.sent:
            copy.wait_send()


def signal(device):
    pl.semaphore_signal(pltpu.get_barrier_semaphore(), inc=1, device_id=device, device_id_type=MESH)


def block_at(position, z):
    return lax.rem(position + 8 - z, 4)


def landed(ref, sem):
    pltpu.make_async_copy(ref, ref, sem).wait()


def nt(a, b):
    return lax.dot_general(a, b, (((1,), (1,)), ((), ())), preferred_element_type=F32)


def tn(a, b):
    return lax.dot_general(a, b, (((0,), (0,)), ((), ())), preferred_element_type=F32)


def nn(a, b):
    return jnp.dot(a, b, preferred_element_type=F32)


def heads(t, lo, q, g, lat, w, gq, d_halo, d_own, kv, gkv, p_t, ds_t, dw_sum, rope_sum):
    rows = q.shape[2]
    block = 2 * rows
    window = 4 * rows
    scale = float(QK) ** -0.5
    pairs = gq.shape[1]
    part = 2 * KV
    quarter = LATENT // 4

    rope_sum[...] = jnp.zeros_like(rope_sum)
    nope = lat[t, :, :, :LATENT].reshape(window, LATENT)
    rope = lat[t, :, :, LATENT:].reshape(window, ROPE)
    lows = lo[t]
    key_at = lax.broadcasted_iota(jnp.int32, (3 * rows, rows), 0)
    query_at = lax.broadcasted_iota(jnp.int32, (3 * rows, rows), 1)

    def project(i, _):
        cols = pl.ds(pl.multiple_of(i * part, part), part)
        kv[:, cols] = nn(nope, w[:, :, cols].reshape(4 * quarter, part)).astype(BF)
        return 0

    lax.fori_loop(0, pairs, project, 0)

    def pair(i, _):
        q_two = q[t, :, :, pl.ds(pl.multiple_of(i * 2 * QK, 2 * QK), 2 * QK)].reshape(block, 2 * QK)
        g_two = g[t, :, :, pl.ds(pl.multiple_of(i * 2 * VDIM, 2 * VDIM), 2 * VDIM)].reshape(block, 2 * VDIM)
        cols = pl.ds(pl.multiple_of(i * part, part), part)
        kv_two = kv[:, cols]
        dq_two, dkv_two = [], []
        for h in range(2):
            qh = q_two[:, h * QK:(h + 1) * QK]
            gh = g_two[:, h * VDIM:(h + 1) * VDIM]
            kh = jnp.concatenate([kv_two[:, h * KV:h * KV + NOPE], rope], axis=1)
            vh = kv_two[:, h * KV + NOPE:(h + 1) * KV]
            scores = nt(kh, qh)
            dprobs = nt(vh, gh)
            for s in range(2):
                keys = slice(rows * s, rows * s + 3 * rows)
                queries = slice(rows * s, rows * s + rows)
                low = lows[:, queries] - rows * s
                seen = (key_at >= low) & (key_at <= query_at + block)
                sc = jnp.where(seen, scores[keys, queries] * scale, LOW)
                top = jnp.max(sc, axis=0, keepdims=True)
                ex = jnp.exp(sc - top)
                probs = ex * (1.0 / jnp.sum(ex, axis=0, keepdims=True))
                probs_low = probs.astype(BF)
                dp = dprobs[keys, queries]
                row_dot = jnp.sum(probs_low.astype(F32) * dp, axis=0, keepdims=True)
                p_t[h, keys, queries] = probs_low
                ds_t[h, keys, queries] = (probs * (dp - row_dot)).astype(BF)
            ds = ds_t[h]
            dq_two.append((tn(ds, kh) * scale).astype(BF))
            dk = nn(ds, qh) * scale
            dv = nn(p_t[h], gh)
            rope_sum[...] += dk[:, NOPE:]
            dkv_two += [dk[:, :NOPE].astype(BF), dv.astype(BF)]
        gkv[:, cols] = jnp.concatenate(dkv_two, axis=1)
        gq[t, i] = jnp.concatenate(dq_two, axis=1).reshape(2, rows, 2 * QK)
        return 0

    lax.fori_loop(0, pairs, pair, 0)

    d_nope = nt(gkv[...], w[...].reshape(4 * quarter, -1)).astype(BF)
    d_rope = rope_sum[...].astype(BF)
    d_halo[t, :, :LATENT] = d_nope[:block]
    d_halo[t, :, LATENT:] = d_rope[:block]
    d_own[t, :, :LATENT] = d_nope[block:]
    d_own[t, :, LATENT:] = d_rope[block:]

    def weight(i, _):
        cols = pl.ds(pl.multiple_of(i * part, part), part)
        dw_sum[:, cols] += tn(nope, gkv[:, cols])
        return 0

    lax.fori_loop(0, pairs, weight, 0)


def main_kernel(
    lo, q, latent, w, g,
    relay, d_latent, d_weight,
    q_all, g_all, lat_all, w_all, gq, d_halo, d_own, dw, d_lat, dw_parts,
    kv, gkv, p_t, ds_t, dw_sum, rope_sum,
    send, recv, w_send, w_recv, w_send2, w_recv2, gq_send, gq_recv, d_send, d_recv, dw_send, dw_recv,
):
    y, x, z, core = place()
    dp = 4 * y + x
    mine = pick(core, x, y)
    other = pick(core, y, x)
    before, after = wrap(z - 1, 8), wrap(z + 1, 8)

    w_axis = lax.rem(z, 2)
    w_first = lax.rem(pick(w_axis, x, y) + 4 - z // 2, 4)
    w_other = pick(w_axis, y, x)
    w_plane = 2 * block_at(mine, z) + core

    for e in range(2):
        half = lax.rem(core + e, 2)
        for d in range(4):
            source = line_dp(core, wrap(mine - d, 4), y, x)
            if d or e:
                signal((source, 2 * z + half))
            signal((source, 2 * before + half))
            axis = 1 - half
            source = line_dp(axis, wrap(pick(axis, x, y) - d, 4), y, x)
            if d or e:
                signal((source, 2 * z + half))
    for d in range(4):
        signal((line_dp(core, wrap(mine - d, 4), y, x), 2 * after + core))
    for b in range(2):
        @pl.when((w_plane != z) | (core != b))
        def _():
            signal((dp, 2 * w_plane + b))

    own_w = jnp.where((w_axis == core) & (lax.rem(z, 4) == w_first), 1, 0)
    pl.semaphore_wait(pltpu.get_barrier_semaphore(), 7 + 8 + 7 + 4 + 2 - own_w)

    moves = Sender()
    quarter = LATENT // 4
    w_width = w.shape[1]
    w_rows = w.at[pl.ds(pl.multiple_of(w_other * quarter, quarter), quarter)]

    def w_slot(part, b):
        return w_all.at[part, :, pl.ds(pl.multiple_of(b * w_width, w_width), w_width)]

    def w_here(i):
        return (w_axis == core) & (w_first + 4 * i == z)

    def w_copy(i):
        return pltpu.make_async_remote_copy(
            src_ref=w_rows, dst_ref=w_slot(w_other, core), send_sem=w_send.at[i], recv_sem=w_recv.at[core],
            device_id=(dp, 2 * (w_first + 4 * i) + w_axis), device_id_type=MESH,
        )

    for i in range(2):
        @pl.when(w_here(i))
        def _():
            pltpu.make_async_copy(w_rows, w_slot(w_other, core), w_recv.at[core]).start()

        @pl.when(jnp.logical_not(w_here(i)))
        def _():
            w_copy(i).start()

    q_width = q.shape[1] // 8
    g_width = g.shape[1] // 8

    def send_rows(d, e):
        axis = lax.rem(core + e, 2)
        spot = pick(axis, x, y)
        there = lax.rem(spot + d, 4)
        target = (line_dp(axis, there, y, x), 2 * z + axis)
        k = 4 * e + d
        at = 2 * block_at(there, z) + axis
        q_part = q.at[:, pl.ds(pl.multiple_of(at * q_width, q_width), q_width)]
        g_part = g.at[:, pl.ds(pl.multiple_of(at * g_width, g_width), g_width)]
        lat_own = lat_all.at[spot, 2 + core]
        if d == 0 and e == 0:
            moves.local(latent, lat_own, recv.at[2, k])
            moves.local(q_part, q_all.at[spot, core], recv.at[0, k])
            moves.local(g_part, g_all.at[spot, core], recv.at[1, k])
        else:
            moves.remote(latent, lat_own, send.at[2, k], recv.at[2, k], target)
            moves.remote(q_part, q_all.at[spot, core], send.at[0, k], recv.at[0, k], target)
            moves.remote(g_part, g_all.at[spot, core], send.at[1, k], recv.at[1, k], target)
        target = (line_dp(axis, there, y, x), 2 * after + axis)
        moves.remote(latent, lat_all.at[spot, core], send.at[3, k], recv.at[3, k], target)

    for d in range(2):
        for e in range(2):
            send_rows(d, e)
    for b in range(2):
        landed(w_slot(other, b), w_recv.at[b])
    for d in range(1, 4):
        target = (line_dp(1 - core, lax.rem(other + d, 4), y, x), 2 * z + core)
        moves.remote(w_all.at[other], w_all.at[other], w_send2.at[d], w_recv2.at[d], target)
    for d in (3, 2):
        for e in range(2):
            send_rows(d, e)
    p_t[...] = jnp.zeros_like(p_t)
    ds_t[...] = jnp.zeros_like(ds_t)
    dw_sum[...] = jnp.zeros_like(dw_sum)
    for d in range(1, 4):
        landed(w_all.at[wrap(other - d, 4)], w_recv2.at[d])

    def gq_copy(s, there, slot, e, d, half):
        return pltpu.make_async_remote_copy(
            src_ref=gq.at[slot, there, half], dst_ref=relay.at[core, other, slot],
            send_sem=gq_send.at[4 * e + d, s], recv_sem=gq_recv.at[4 * e + d, s],
            device_id=(line_dp(1 - core, there, y, x), 2 * z + half), device_id_type=MESH,
        )

    def d_copy(s, slot, kind):
        target = (line_dp(core, slot, y, x), 2 * (z if kind == 0 else before) + core)
        return pltpu.make_async_remote_copy(
            src_ref=(d_own, d_halo)[kind].at[slot], dst_ref=d_lat.at[kind, mine],
            send_sem=d_send.at[kind, s], recv_sem=d_recv.at[kind, s],
            device_id=target, device_id_type=MESH,
        )

    def order(s):
        return s + (s // 2) * (1 - 2 * lax.rem(s, 2))

    def step(s, _):
        d = order(s)
        slot = lax.rem(mine + 4 - d, 4)
        for e in range(2):
            k = 4 * e + d
            half = lax.rem(core + e, 2)
            landed(q_all.at[slot, half], recv.at[0, k])
            landed(g_all.at[slot, half], recv.at[1, k])
            landed(lat_all.at[slot, 2 + half], recv.at[2, k])
            landed(lat_all.at[slot, half], recv.at[3, k])
        heads(slot, lo, q_all, g_all, lat_all, w_all, gq, d_halo, d_own, kv, gkv, p_t, ds_t, dw_sum, rope_sum)
        for dm in (2, 1, 3, 0):
            there = lax.rem(other + dm, 4)
            for e in range(2):
                half = lax.rem(core + e, 2)
                if dm == 0 and e == 0:
                    pltpu.make_async_copy(
                        gq.at[slot, there, half], relay.at[core, other, slot], gq_recv.at[0, s]
                    ).start()
                else:
                    gq_copy(s, there, slot, e, dm, half).start()
        d_copy(s, slot, 1).start()

        @pl.when(s == 0)
        def _():
            pltpu.make_async_copy(d_own.at[slot], d_lat.at[0, mine], d_recv.at[0, s]).start()

        @pl.when(s > 0)
        def _():
            d_copy(s, slot, 0).start()

        return 0

    lax.fori_loop(0, 4, step, 0)

    dw[...] = dw_sum[...].astype(BF).reshape(dw.shape)
    for d in (2, 1, 3, 0):
        there = lax.rem(other + d, 4)
        if d == 0:
            late = pltpu.make_async_copy(dw.at[there], dw_parts.at[other], dw_recv.at[d])
            late.start()
        else:
            target = (line_dp(1 - core, there, y, x), 2 * z + core)
            late = pltpu.make_async_remote_copy(
                src_ref=dw.at[there], dst_ref=dw_parts.at[other], send_sem=dw_send.at[d], recv_sem=dw_recv.at[d],
                device_id=target, device_id_type=MESH,
            )
            late.start()

    def collect(s, _):
        d = order(s)
        landed(d_lat.at[0, lax.rem(mine + d, 4)], d_recv.at[0, s])
        landed(d_lat.at[1, lax.rem(mine + d, 4)], d_recv.at[1, s])
        return 0

    lax.fori_loop(0, 4, collect, 0)
    total = jnp.zeros(d_latent.shape, F32)
    for kind in range(2):
        for i in range(4):
            total += d_lat[kind, i].astype(F32)
    d_latent[...] = total
    for d in range(4):
        landed(dw_parts.at[lax.rem(other + 4 - d, 4)], dw_recv.at[d])
    total = jnp.zeros(d_weight.shape, F32)
    for i in range(4):
        total += dw_parts[i].astype(F32)
    d_weight[...] = total

    for copy in moves.sent:
        copy.wait_send()
    for i in range(2):
        @pl.when(jnp.logical_not(w_here(i)))
        def _():
            w_copy(i).wait_send()
    for d in range(1, 4):
        landed(dw.at[lax.rem(other + d, 4)], dw_send.at[d])

    def close(s, _):
        d = order(s)
        slot = lax.rem(mine + 4 - d, 4)
        for dm in range(4):
            for e in range(2):
                landed(relay.at[core, other, slot], gq_recv.at[4 * e + dm, s])
                if dm or e:
                    landed(gq.at[slot, 0, 0], gq_send.at[4 * e + dm, s])
        landed(d_halo.at[slot], d_send.at[1, s])

        @pl.when(s > 0)
        def _():
            landed(d_own.at[slot], d_send.at[0, s])

        return 0

    lax.fori_loop(0, 4, close, 0)


def main_part(lo, q, latent, w, g):
    rows = q.shape[0]
    block, window = 2 * rows, 4 * rows
    q_width, g_width, w_width = q.shape[1] // 8, g.shape[1] // 8, 2 * w.shape[1]
    pairs = q_width // (2 * QK)
    dma = pltpu.SemaphoreType.DMA
    vmem = pl.BlockSpec(memory_space=pltpu.VMEM)
    return pl.pallas_call(
        main_kernel,
        out_shape=[
            jax.ShapeDtypeStruct((2, 4, 4, rows, 2 * QK), BF),
            jax.ShapeDtypeStruct((block, WIDE), F32),
            jax.ShapeDtypeStruct((LATENT // 4, w_width), F32),
        ],
        in_specs=[vmem] + [ANY] * 4,
        out_specs=[ANY, vmem, vmem],
        scratch_shapes=[
            pltpu.VMEM((4, 2, rows, q_width), BF),
            pltpu.VMEM((4, 2, rows, g_width), BF),
            pltpu.VMEM((4, 4, rows, WIDE), BF),
            pltpu.VMEM((4, LATENT // 4, w_width), BF),
            pltpu.VMEM((4, pairs, 2, rows, 2 * QK), BF),
            pltpu.VMEM((4, block, WIDE), BF),
            pltpu.VMEM((4, block, WIDE), BF),
            pltpu.VMEM((4, LATENT // 4, w_width), BF),
            pltpu.VMEM((2, 4, block, WIDE), BF),
            pltpu.VMEM((4, LATENT // 4, w_width), BF),
            pltpu.VMEM((window, w_width), BF),
            pltpu.VMEM((window, w_width), BF),
            pltpu.VMEM((2, window, block), BF),
            pltpu.VMEM((2, window, block), BF),
            pltpu.VMEM((LATENT, w_width), F32),
            pltpu.VMEM((window, ROPE), F32),
            dma((4, 8)), dma((4, 8)), dma((2,)), dma((2,)), dma((4,)), dma((4,)),
            dma((8, 4)), dma((8, 4)), dma((2, 4)), dma((2, 4)), dma((4,)), dma((4,)),
        ],
        compiler_params=pltpu.CompilerParams(
            collective_id=0, has_side_effects=True, vmem_limit_bytes=56 * 1024 * 1024
        ),
        name="heads_and_exchanges",
    )(lo, q, latent, w, g)


def deliver_kernel(chosen, d_lat, dw, gq, lat_relay, dw_parts, send, recv, send2, recv2, send3, recv3):
    y, x, z, core = place()
    dp = 4 * y + x
    ctx = 2 * z + core
    for d in range(16):
        there = lax.rem(dp + d, 16)
        if d:
            signal((there, ctx))
        signal((there, 2 * z + 1 - core))
    mine = pick(core, x, y)
    part = block_at(mine, z)

    def dw_home(plane):
        return line_dp(core, lax.rem(part + plane, 4), y, x), 2 * plane + core

    for d in range(1, 8):
        signal(dw_home(lax.rem(z + d, 8)))
    pl.semaphore_wait(pltpu.get_barrier_semaphore(), 38)

    moves = Sender()
    width = chosen.shape[3]
    for d in range(16):
        there = lax.rem(dp + d, 16)
        for e in range(2):
            half = lax.rem(core + e, 2)
            src, dst = d_lat.at[half, there], lat_relay.at[dp, core]
            if d == 0 and e == 0:
                moves.local(src, dst, recv2.at[e, d])
            else:
                moves.remote(src, dst, send2.at[e, d], recv2.at[e, d], (there, 2 * z + half))
    for d in range(16):
        there = lax.rem(dp + d, 16)
        for j, at in ((0, 8 * block_at(x, z) + y), (1, 8 * block_at(y, z) + 4 + x)):
            dst = gq.at[:, pl.ds(pl.multiple_of(at * width, width), width)]
            if d == 0:
                moves.local(chosen.at[there, j], dst, recv.at[j, d])
            else:
                moves.remote(chosen.at[there, j], dst, send.at[j, d], recv.at[j, d], (there, ctx))
    for d in range(8):
        there = lax.rem(z + d, 8)
        if d == 0:
            moves.local(dw.at[there], dw_parts.at[z], recv3.at[d])
        else:
            moves.remote(dw.at[there], dw_parts.at[z], send3.at[d], recv3.at[d], dw_home(there))
    moves.finish()


def deliver(chosen, d_lat, dw):
    _, _, rows, width = chosen.shape
    return pl.pallas_call(
        deliver_kernel,
        out_shape=[
            jax.ShapeDtypeStruct((rows, 32 * width), BF),
            jax.ShapeDtypeStruct((16, 2) + d_lat.shape[2:], F32),
            jax.ShapeDtypeStruct(dw.shape, F32),
        ],
        in_specs=[ANY] * 3,
        out_specs=[ANY] * 3,
        scratch_shapes=[
            pltpu.SemaphoreType.DMA((2, 16)),
            pltpu.SemaphoreType.DMA((2, 16)),
            pltpu.SemaphoreType.DMA((2, 16)),
            pltpu.SemaphoreType.DMA((2, 16)),
            pltpu.SemaphoreType.DMA((8,)),
            pltpu.SemaphoreType.DMA((8,)),
        ],
        compiler_params=pltpu.CompilerParams(collective_id=2, has_side_effects=True),
        name="deliver_queries",
    )(chosen, d_lat, dw)


def weight_home(k):
    pairs = []
    for dp in range(16):
        for ctx in range(16):
            y, x, z, core = dp // 4, dp % 4, ctx // 2, ctx % 2
            mine, other = (x, y) if core == 0 else (y, x)
            piece = k ^ (z % 2)
            home = (4 * other + z // 2) * 16 + 4 * ((mine - z) % 4) + 2 * core + piece
            pairs.append((dp * 16 + ctx, home))
    return pairs


def body(queries, latent, w_kv, grad_out, doc_lengths, matching):
    y, x, z, core = place()
    dp = 4 * y + x
    rows = queries.shape[0]
    block = 2 * rows

    packs = pick(core, 4 * y + jnp.arange(4), 4 * jnp.arange(4) + x)
    ends = jnp.cumsum(doc_lengths[packs], axis=1)
    token = z * block + jnp.arange(block, dtype=jnp.int32)
    begun = jnp.where(ends[:, None, :] <= token[None, :, None], ends[:, None, :], 0)
    lo = (jnp.max(begun, axis=2) - (z - 1) * block)[:, None, :].astype(jnp.int32)

    relay, d_lat, dw_mine = main_part(lo, queries, latent, w_kv, grad_out)

    major, minor = matching // 4, lax.rem(matching, 4)
    chosen = jnp.stack([relay[0][major, minor], relay[1][minor, major]], axis=1)
    d_lat = d_lat.reshape(2, 16, rows // 16, WIDE)
    dw_mine = dw_mine.reshape(8, LATENT // 32, dw_mine.shape[1])
    grad_queries, lat_relay, dw_z = deliver(chosen, d_lat, dw_mine)

    lat_chosen = jnp.sum(lat_relay, axis=1)[matching]
    grad_latent = lax.all_to_all(lat_chosen, "dp", split_axis=0, concat_axis=0, tiled=True).reshape(rows, WIDE)

    dw_last = jnp.sum(dw_z, axis=0).reshape(LATENT // 32, 2, -1)
    odd = lax.rem(z, 2)
    arrived = [
        lax.ppermute(jnp.where(odd == k, dw_last[:, 0], dw_last[:, 1]), ("dp", "ctx"), weight_home(k))
        for k in range(2)
    ]
    grad_weight = jnp.concatenate(
        [jnp.where(core == 0, arrived[0], arrived[1]), jnp.where(core == 0, arrived[1], arrived[0])], axis=0
    )
    return grad_queries, grad_latent, grad_weight


def solution(mesh):
    in_specs = (
        P(("dp", "ctx"), None),
        P(("dp", "ctx"), None),
        P(None, "ctx"),
        P(("dp", "ctx"), None),
        P(),
        P(),
    )
    out_specs = (P(("dp", "ctx"), None), P(("dp", "ctx"), None), P("dp", "ctx"))
    return jax.shard_map(body, mesh=mesh, in_specs=in_specs, out_specs=out_specs, check_vma=False)
```

time: 284 us -> 248 us (0.87)
  Pallas kernels: 234 us -> 204 us
    pallas_call x3 -> x1, Pallas kernels: 172 us -> 130 us  [main_part(): pl.pallas_call(main_kernel, out_shape=[jax.ShapeDtypeStruct((2, 4, 4, row...]
    pallas_call x1, Pallas kernels: 61.2 us -> 73.9 us  [deliver(): pl.pallas_call(deliver_kernel, out_shape=[jax.ShapeDtypeStruct((rows, 32...]
    ppermute x2, starting transfers between devices: 6.41 us -> 1.92 us  [body(): lax.ppermute(jnp.where(odd == k, dw_last[:, 0], dw_last[:, 1]), ('dp', 'c...]
    unnamed x20 -> x12, local copies, waits for them, and re-layouts: 8.39 us -> 5.53 us
where the time goes in v2:
time: 248 us; the launch traced here: 246 us
  Pallas kernels  204 us (82%)
  local copies, waits for them, and re-layouts  14.2 us (6%)
  starting transfers between devices  12 us (5%)
  other arithmetic  8.07 us (3%)
  waiting for transfers between devices  6.32 us (3%)
    pallas_call x1, Pallas kernels, main_part(): pl.pallas_call(main_kernel, out_shape=[jax.ShapeDtypeStruct((2, 4, 4, row...  130 us
    pallas_call x1, Pallas kernels, deliver(): pl.pallas_call(deliver_kernel, out_shape=[jax.ShapeDtypeStruct((rows, 32...  73.9 us
    all_to_all x1, starting transfers between devices, body(): lax.all_to_all(lat_chosen, 'dp', split_axis=0, concat_axis=0, tiled=True)  10 us
    all_to_all x1, waiting for transfers between devices, body(): lax.all_to_all(lat_chosen, 'dp', split_axis=0, concat_axis=0, tiled=True)  6.31 us
    unnamed x12, local copies, waits for them, and re-layouts  5.53 us
  transfers between devices with their start and end apart: 3, of which 1 were waited for; matrix products, arithmetic and copies ran while one was open for 2% of the time, Pallas kernels for 0%

profile of v2, /device:TPU:1, one launch (start us, length us, event | category | flops | bytes accessed | tf_op | source)
XLA Modules:
  0.0 245.6 jit_solution(11223005238142087918)
XLA Ops:
  0.6 0.0 copy-start
  0.7 0.6 copy-done
  1.3 0.6 gather_fusion
  1.9 0.2 reduce_window_sum.11
  2.1 0.1 select_reduce_fusion
  2.2 0.6 sub.39.lo
  2.8 1.7 copy.15.latent
  4.5 130.3 %heads_and_exchanges.1 = (bf16[2,4,4,128,384]{4,3,2,1,0:T(8,128)(2,1)}, f32[256,576]{1,0:T(8,128)}, f32[128,2048]{1,0:T(8,128)}) custom-call(s32[4,1,256]{2,1,0:T(1,128)} %sub.39.lo, bf16[128,12288]{1,0:T(8,128)(2,1)} %q.1, bf16[128,576]{1,0:T(8,128)(2,1)} %copy.15.latent, bf16[512,1024]{1,0:T(8,128)(2,1)} %w.1, bf16[128,8192]{1,0:T(8,128)(2,1)} %g.1), custom_call_target="tpu_custom_call" | custom-call | tf_op jit(solution)/shard_map/heads_and_exchanges/pallas_call | solution.py:399
  134.8 0.0 copy-start.3
  134.8 2.2 slice_bitcast_fusion.1
  137.0 0.0 copy-done.3
  137.1 1.9 gather_fusion.2
  139.0 1.9 gather_fusion.1
  140.9 0.0 copy-done.1
  140.9 3.4 %pad_maximum_fusion.chosen = bf16[16,2,128,384]{3,2,1,0:T(8,128)(2,1)} fusion(bf16[16,1,128,384]{3,2,1,0:T(8,128)(2,1)S(1)} %bitcast.16, bf16[16,1,128,384]{3,2,1,0:T(8,128)(2,1)} %bitcast.17), kind=kLoop, calls=%fused_computation.4 | loop fusion | flops 1572864 | bytes 6291456 | tf_op jit(solution)/shard_map/stack | solution.py:533
  144.4 73.9 %deliver_queries.1 = (bf16[128,12288]{1,0:T(8,128)(2,1)}, f32[16,2,8,576]{3,2,1,0:T(8,128)}, f32[8,16,2048]{2,1,0:T(8,128)}) custom-call(bf16[16,2,128,384]{3,2,1,0:T(8,128)(2,1)} %pad_maximum_fusion.chosen, f32[2,16,8,576]{3,2,1,0:T(8,128)} %bitcast.20, f32[8,16,2048]{2,1,0:T(8,128)} %bitcast.19), custom_call_target="tpu_custom_call" | custom-call | tf_op jit(solution)/shard_map/deliver_queries/pallas_call | solution.py:484
  218.3 1.3 reduce_sum.19
  219.6 0.1 reshape.76
  219.7 0.1 fusion.5
  219.9 1.9 collective-permute-start
  221.8 0.6 copy.27
  222.5 0.0 collective-permute-start.1
  222.5 1.3 reduce_sum.18
  223.8 1.3 gather_fusion.3
  225.1 10.0 %all-to-all-start = ((f32[16,8,576]{2,1,0:T(8,128)}), f32[16,8,576]{2,1,0:T(8,128)S(1)}, u32[]{:S(2)}, u32[]{:S(2)}) async-start(f32[16,8,576]{2,1,0:T(8,128)} %gather_fusion.3), calls=%async_computation | async-start | bytes 655360 | tf_op jit(solution)/shard_map/all_to_all | solution.py:539
  235.1 0.0 collective-permute-done
  235.1 0.0 collective-permute-done.1
  235.2 0.9 broadcast_select_fusion.2
  236.0 0.7 pad_maximum_fusion.1
  236.7 6.3 %all-to-all-done = f32[16,8,576]{2,1,0:T(8,128)S(1)} async-done(((f32[16,8,576]{2,1,0:T(8,128)}), f32[16,8,576]{2,1,0:T(8,128)S(1)}, u32[]{:S(2)}, u32[]{:S(2)}) %all-to-all-start) | async-done | bytes 294944 | tf_op jit(solution)/shard_map/all_to_all | solution.py:539
  243.0 0.9 copy.19
  243.9 1.7 copy.29
  (11 shorter events, 0.1 us)
Async XLA Ops:
  0.6 0.7 copy-start
  134.8 2.3 copy-start.3
  139.0 1.9 copy-start.1
  219.9 15.3 %collective-permute-start = (f32[16,1024]{1,0:T(8,128)S(1)}, f32[16,1024]{1,0:T(8,128)}, u32[]{:S(2)}, u32[]{:S(2)}) collective-permute-start(f32[16,1024]{1,0:T(8,128)S(1)} %fusion), channel_id=1, source_target_pairs={{0,0},{1,2},{2,13},{3,15},{4,24},{5,26},{6,21},{7,23},{8,32},{9,34... | collective-permute-start | bytes 196616 | tf_op jit(solution)/shard_map/ppermute | solution.py:544
  222.5 12.7 %collective-permute-start.1 = (f32[16,1024]{1,0:T(8,128)}, f32[16,1024]{1,0:T(8,128)}, u32[]{:S(2)}, u32[]{:S(2)}) collective-permute-start(f32[16,1024]{1,0:T(8,128)} %bitcast.15), channel_id=1, source_target_pairs={{0,1},{1,3},{2,12},{3,14},{4,25},{5,27},{6,20},{7,22},{8,33},{9,35... | collective-permute-start | bytes 196616 | tf_op jit(solution)/shard_map/ppermute | solution.py:544
  222.5 21.4 %copy-start.2 = (bf16[128,12288]{1,0:T(8,128)(2,1)S(1)}, bf16[128,12288]{1,0:T(8,128)(2,1)}, u32[]{:S(2)}) copy-start(bf16[128,12288]{1,0:T(8,128)(2,1)} %get-tuple-element.35) | copy-start | bytes 9437188
  225.1 17.9 %all-to-all-start = ((f32[16,8,576]{2,1,0:T(8,128)}), f32[16,8,576]{2,1,0:T(8,128)S(1)}, u32[]{:S(2)}, u32[]{:S(2)}) async-start(f32[16,8,576]{2,1,0:T(8,128)} %gather_fusion.3), calls=%async_computation | async-start | bytes 655360 | tf_op jit(solution)/shard_map/all_to_all | solution.py:539

commit v3 on v2

v3 whole, which is shorter than its diff:
```python
import jax
import jax.numpy as jnp
from jax import lax
from jax.experimental import pallas as pl
from jax.experimental.pallas import tpu as pltpu
from jax.sharding import PartitionSpec as P

NOPE = 128
ROPE = 64
VDIM = 128
LATENT = 512
HEADS = 64
ROWS = 128
QK = NOPE + ROPE
KV = NOPE + VDIM
WIDE = LATENT + ROPE
MESH = pl.DeviceIdType.MESH
ANY = pl.BlockSpec(memory_space=pl.ANY)
BF = jnp.bfloat16
F32 = jnp.float32
LOW = -1e30


def place():
    dp, ctx = lax.axis_index("dp"), lax.axis_index("ctx")
    return dp // 4, lax.rem(dp, 4), ctx // 2, lax.rem(ctx, 2)


def pick(axis, on_x, on_y):
    return (1 - axis) * on_x + axis * on_y


def wrap(value, n):
    return lax.rem(value + n, n)


def line_dp(axis, position, y, x):
    return pick(axis, 4 * y + position, 4 * position + x)


class Sender:
    def __init__(self):
        self.sent = []
        self.due = []

    def remote(self, src, dst, send_sem, recv_sem, device):
        copy = pltpu.make_async_remote_copy(
            src_ref=src, dst_ref=dst, send_sem=send_sem, recv_sem=recv_sem,
            device_id=device, device_id_type=MESH,
        )
        copy.start()
        self.sent.append(copy)
        return copy

    def local(self, src, dst, sem):
        copy = pltpu.make_async_copy(src, dst, sem)
        copy.start()
        self.due.append(copy)


def signal(device):
    pl.semaphore_signal(pltpu.get_barrier_semaphore(), inc=1, device_id=device, device_id_type=MESH)


def block_at(position, z):
    return lax.rem(position + 8 - z, 4)


def landed(ref, sem):
    pltpu.make_async_copy(ref, ref, sem).wait()


def nt(a, b):
    return lax.dot_general(a, b, (((1,), (1,)), ((), ())), preferred_element_type=F32)


def tn(a, b):
    return lax.dot_general(a, b, (((0,), (0,)), ((), ())), preferred_element_type=F32)


def nn(a, b):
    return jnp.dot(a, b, preferred_element_type=F32)


def heads(t, lo, q, g, lat, w, gq, d_halo, d_own, kv, gkv, p_t, ds_t, dw_sum, rope_sum):
    rows = q.shape[2]
    block = 2 * rows
    window = 4 * rows
    scale = float(QK) ** -0.5
    pairs = gq.shape[1]
    part = 2 * KV
    quarter = LATENT // 4

    rope_sum[...] = jnp.zeros_like(rope_sum)
    nope = lat[t, :, :, :LATENT].reshape(window, LATENT)
    rope = lat[t, :, :, LATENT:].reshape(window, ROPE)
    lows = lo[t]
    key_at = lax.broadcasted_iota(jnp.int32, (3 * rows, rows), 0)
    query_at = lax.broadcasted_iota(jnp.int32, (3 * rows, rows), 1)

    def project(i, _):
        cols = pl.ds(pl.multiple_of(i * part, part), part)
        kv[:, cols] = nn(nope, w[:, :, cols].reshape(4 * quarter, part)).astype(BF)
        return 0

    lax.fori_loop(0, pairs, project, 0)

    def pair(i, _):
        q_two = q[t, :, :, pl.ds(pl.multiple_of(i * 2 * QK, 2 * QK), 2 * QK)].reshape(block, 2 * QK)
        g_two = g[t, :, :, pl.ds(pl.multiple_of(i * 2 * VDIM, 2 * VDIM), 2 * VDIM)].reshape(block, 2 * VDIM)
        cols = pl.ds(pl.multiple_of(i * part, part), part)
        kv_two = kv[:, cols]
        dq_two, dkv_two = [], []
        for h in range(2):
            qh = q_two[:, h * QK:(h + 1) * QK]
            gh = g_two[:, h * VDIM:(h + 1) * VDIM]
            kh = jnp.concatenate([kv_two[:, h * KV:h * KV + NOPE], rope], axis=1)
            vh = kv_two[:, h * KV + NOPE:(h + 1) * KV]
            scores = nt(kh, qh)
            dprobs = nt(vh, gh)
            for s in range(2):
                keys = slice(rows * s, rows * s + 3 * rows)
                queries = slice(rows * s, rows * s + rows)
                low = lows[:, queries] - rows * s
                seen = (key_at >= low) & (key_at <= query_at + block)
                sc = jnp.where(seen, scores[keys, queries] * scale, LOW)
                top = jnp.max(sc, axis=0, keepdims=True)
                ex = jnp.exp(sc - top)
                probs = ex * (1.0 / jnp.sum(ex, axis=0, keepdims=True))
                probs_low = probs.astype(BF)
                dp = dprobs[keys, queries]
                row_dot = jnp.sum(probs_low.astype(F32) * dp, axis=0, keepdims=True)
                p_t[h, keys, queries] = probs_low
                ds_t[h, keys, queries] = (probs * (dp - row_dot)).astype(BF)
            ds = ds_t[h]
            dq_two.append((tn(ds, kh) * scale).astype(BF))
            dk = nn(ds, qh) * scale
            dv = nn(p_t[h], gh)
            rope_sum[...] += dk[:, NOPE:]
            dkv_two += [dk[:, :NOPE].astype(BF), dv.astype(BF)]
        gkv[:, cols] = jnp.concatenate(dkv_two, axis=1)
        gq[t, i] = jnp.concatenate(dq_two, axis=1).reshape(2, rows, 2 * QK)
        return 0

    lax.fori_loop(0, pairs, pair, 0)

    d_nope = nt(gkv[...], w[...].reshape(4 * quarter, -1))
    d_halo[t, :, :LATENT] = d_nope[:block].astype(BF)
    d_halo[t, :, LATENT:] = rope_sum[:block].astype(BF)
    d_own[t, :, :LATENT] = d_nope[block:]
    d_own[t, :, LATENT:] = rope_sum[block:]

    def weight(i, _):
        cols = pl.ds(pl.multiple_of(i * part, part), part)
        dw_sum[:, cols] += tn(nope, gkv[:, cols])
        return 0

    lax.fori_loop(0, pairs, weight, 0)


def main_kernel(
    lo, from_x, from_y, q, latent, w, g,
    grad_q, grad_lat, grad_w,
    q_all, g_all, lat_all, w_all, gq, relay, chosen, come,
    d_halo, d_in, d_own, d_line, d_lat, d_sum, d_relay, d_pick,
    dw, dw_parts, dw_total, dw_z, dw_last,
    kv, gkv, p_t, ds_t, dw_sum, rope_sum,
    send, recv, w_send, w_recv, w_send2, w_recv2, z_send, z_recv, gq_send, gq_recv, d_send, d_recv,
    a_send, a_recv, b_send, b_recv, r_send, r_recv, out_sem, dw_send, dw_recv, dz_send, dz_recv, dl_send, dl_recv,
):
    y, x, z, core = place()
    dp = 4 * y + x
    ctx = 2 * z + core
    mine = pick(core, x, y)
    other = pick(core, y, x)
    before, after = wrap(z - 1, 8), wrap(z + 1, 8)
    rows = q.shape[0]
    quarter = LATENT // 4
    w_width = w.shape[1]

    w_axis = lax.rem(z, 2)
    w_first = lax.rem(pick(w_axis, x, y) + 4 - z // 2, 4)
    w_other = pick(w_axis, y, x)
    part = block_at(mine, z)
    w_plane = 2 * part + core

    def dw_mate(plane):
        return line_dp(core, lax.rem(part + plane, 4), y, x), 2 * plane + core

    def dw_home(b):
        return 4 * other + z // 2, 2 * w_plane + b

    def dw_source(odd):
        plane = 2 * x + odd
        spot = lax.rem(z // 2 + plane, 4)
        return pick(w_axis, 4 * y + spot, 4 * spot + y), 2 * plane + w_axis

    def is_me(device):
        return (device[0] == dp) & (device[1] == ctx)

    for d in range(16):
        there = lax.rem(dp + d, 16)
        if d:
            signal((there, ctx))
        signal((there, 2 * z + 1 - core))
    signal((dp, 2 * before + core))
    signal((dp, 2 * after + core))
    for d in range(1, 8):
        signal(dw_mate(lax.rem(z + d, 8)))
    strangers = 0
    for b in range(2):
        @pl.when(jnp.logical_not(is_me((dp, 2 * w_plane + b))))
        def _():
            signal((dp, 2 * w_plane + b))

        @pl.when(jnp.logical_not(is_me(dw_source(b))))
        def _():
            signal(dw_source(b))

        strangers += jnp.where(is_me((dp, 2 * (w_first + 4 * b) + w_axis)), 0, 1)
        strangers += jnp.where(is_me(dw_home(b)), 0, 1)

    pl.semaphore_wait(pltpu.get_barrier_semaphore(), 31 + 2 + 7 + strangers)

    moves = Sender()
    w_rows = w.at[pl.ds(pl.multiple_of(w_other * quarter, quarter), quarter)]

    def w_slot(at, b):
        return w_all.at[at, :, pl.ds(pl.multiple_of(b * w_width, w_width), w_width)]

    def w_here(i):
        return is_me((dp, 2 * (w_first + 4 * i) + w_axis))

    def w_copy(i):
        return pltpu.make_async_remote_copy(
            src_ref=w_rows, dst_ref=w_slot(w_other, core), send_sem=w_send.at[i], recv_sem=w_recv.at[core],
            device_id=(dp, 2 * (w_first + 4 * i) + w_axis), device_id_type=MESH,
        )

    for i in range(2):
        @pl.when(w_here(i))
        def _():
            pltpu.make_async_copy(w_rows, w_slot(w_other, core), w_recv.at[core]).start()

        @pl.when(jnp.logical_not(w_here(i)))
        def _():
            w_copy(i).start()

    q_width = q.shape[1] // 8
    g_width = g.shape[1] // 8

    def send_latent(d, e):
        axis = lax.rem(core + e, 2)
        spot = pick(axis, x, y)
        k = 4 * e + d
        dst = lat_all.at[spot, 2 + core]
        if d == 0 and e == 0:
            moves.local(latent, dst, recv.at[2, k])
        else:
            target = (line_dp(axis, lax.rem(spot + d, 4), y, x), 2 * z + axis)
            moves.remote(latent, dst, send.at[2, k], recv.at[2, k], target)

    def send_rows(d, e):
        axis = lax.rem(core + e, 2)
        spot = pick(axis, x, y)
        there = lax.rem(spot + d, 4)
        target = (line_dp(axis, there, y, x), 2 * z + axis)
        k = 4 * e + d
        at = 2 * block_at(there, z) + axis
        q_part = q.at[:, pl.ds(pl.multiple_of(at * q_width, q_width), q_width)]
        g_part = g.at[:, pl.ds(pl.multiple_of(at * g_width, g_width), g_width)]
        if d == 0 and e == 0:
            moves.local(q_part, q_all.at[spot, core], recv.at[0, k])
            moves.local(g_part, g_all.at[spot, core], recv.at[1, k])
        else:
            moves.remote(q_part, q_all.at[spot, core], send.at[0, k], recv.at[0, k], target)
            moves.remote(g_part, g_all.at[spot, core], send.at[1, k], recv.at[1, k], target)

    def forward_latent(d):
        slot = wrap(mine - d, 4)
        for e in range(2):
            landed(lat_all.at[slot, 2 + lax.rem(core + e, 2)], recv.at[2, 4 * e + d])
        moves.remote(
            lat_all.at[slot, pl.ds(2, 2)], lat_all.at[slot, pl.ds(0, 2)],
            z_send.at[0, d], z_recv.at[0, d], (dp, 2 * after + core),
        )

    for d in range(4):
        for e in range(2):
            send_latent(d, e)
    for d in range(2):
        for e in range(2):
            send_rows(d, e)
    forward_latent(0)
    for b in range(2):
        landed(w_slot(other, b), w_recv.at[b])
    for d in range(1, 4):
        target = (line_dp(1 - core, lax.rem(other + d, 4), y, x), 2 * z + core)
        moves.remote(w_all.at[other], w_all.at[other], w_send2.at[d], w_recv2.at[d], target)
    for d in (3, 2):
        for e in range(2):
            send_rows(d, e)
    for d in (1, 3, 2):
        forward_latent(d)
    p_t[...] = jnp.zeros_like(p_t)
    ds_t[...] = jnp.zeros_like(ds_t)
    dw_sum[...] = jnp.zeros_like(dw_sum)
    for d in range(1, 4):
        landed(w_all.at[wrap(other - d, 4)], w_recv2.at[d])

    def gq_copy(s, there, slot, e, d, half):
        return pltpu.make_async_remote_copy(
            src_ref=gq.at[slot, there, half], dst_ref=relay.at[core, 4 * other + slot],
            send_sem=gq_send.at[4 * e + d, s], recv_sem=gq_recv.at[4 * e + d, s],
            device_id=(line_dp(1 - core, there, y, x), 2 * z + half), device_id_type=MESH,
        )

    def halo_copy(s, slot):
        return pltpu.make_async_remote_copy(
            src_ref=d_halo.at[slot], dst_ref=d_in.at[slot], send_sem=z_send.at[1, s], recv_sem=z_recv.at[1, s],
            device_id=(dp, 2 * before + core), device_id_type=MESH,
        )

    def d_copy(s, slot):
        return pltpu.make_async_remote_copy(
            src_ref=d_line.at[slot], dst_ref=d_lat.at[mine], send_sem=d_send.at[s], recv_sem=d_recv.at[s],
            device_id=(line_dp(core, slot, y, x), 2 * z + core), device_id_type=MESH,
        )

    def order(s):
        return s + (s // 2) * (1 - 2 * lax.rem(s, 2))

    def slot_of(s):
        return lax.rem(mine + 4 - order(s), 4)

    def add_halo(s):
        slot = slot_of(s)
        landed(d_in.at[slot], z_recv.at[1, s])
        d_line[slot] = (d_own[slot] + d_in[slot].astype(F32)).astype(BF)

        @pl.when(s == 0)
        def _():
            pltpu.make_async_copy(d_line.at[slot], d_lat.at[mine], d_recv.at[s]).start()

        @pl.when(s > 0)
        def _():
            d_copy(s, slot).start()

    def step(s, _):
        d = order(s)
        slot = slot_of(s)
        for e in range(2):
            half = lax.rem(core + e, 2)
            landed(q_all.at[slot, half], recv.at[0, 4 * e + d])
            landed(g_all.at[slot, half], recv.at[1, 4 * e + d])
        landed(lat_all.at[slot, pl.ds(0, 2)], z_recv.at[0, d])
        heads(slot, lo, q_all, g_all, lat_all, w_all, gq, d_halo, d_own, kv, gkv, p_t, ds_t, dw_sum, rope_sum)
        halo_copy(s, slot).start()
        for dm in (2, 1, 3, 0):
            there = lax.rem(other + dm, 4)
            for e in range(2):
                half = lax.rem(core + e, 2)
                if dm == 0 and e == 0:
                    pltpu.make_async_copy(
                        gq.at[slot, there, half], relay.at[core, 4 * other + slot], gq_recv.at[0, s]
                    ).start()
                else:
                    gq_copy(s, there, slot, e, dm, half).start()

        @pl.when(s > 0)
        def _():
            add_halo(s - 1)

        return 0

    lax.fori_loop(0, 4, step, 0)

    dw[...] = dw_sum[...].astype(BF).reshape(dw.shape)
    for d in (2, 1, 3, 0):
        there = lax.rem(other + d, 4)
        if d == 0:
            moves.local(dw.at[there], dw_parts.at[other], dw_recv.at[d])
        else:
            target = (line_dp(1 - core, there, y, x), 2 * z + core)
            moves.remote(dw.at[there], dw_parts.at[other], dw_send.at[d], dw_recv.at[d], target)
    add_halo(jnp.int32(3))

    def relayed(s, _):
        for k in range(8):
            landed(relay.at[core, 4 * other], gq_recv.at[k, s])
        return 0

    lax.fori_loop(0, 4, relayed, 0)

    def deliver(d):
        there = lax.rem(dp + d, 16)
        chosen[there, 0] = relay[0, from_x[there]]
        chosen[there, 1] = relay[1, from_y[there]]
        if d == 0:
            moves.local(chosen.at[there], come.at[dp], r_recv.at[d])
        else:
            moves.remote(chosen.at[there], come.at[dp], r_send.at[d], r_recv.at[d], (there, ctx))

    for d in range(15, -1, -1):
        deliver(d)

    def collect(s, _):
        landed(d_lat.at[lax.rem(mine + order(s), 4)], d_recv.at[s])
        return 0

    lax.fori_loop(0, 4, collect, 0)
    total = d_lat[0].astype(F32)
    for i in range(1, 4):
        total += d_lat[i].astype(F32)
    d_sum[...] = total.reshape(d_sum.shape)
    for d in range(16):
        there = lax.rem(dp + d, 16)
        for e in range(2):
            half = lax.rem(core + e, 2)
            if d == 0 and e == 0:
                moves.local(d_sum.at[half, there], d_relay.at[dp, core], a_recv.at[e, d])
            else:
                moves.remote(
                    d_sum.at[half, there], d_relay.at[dp, core], a_send.at[e, d], a_recv.at[e, d],
                    (there, 2 * z + half),
                )

    for d in range(4):
        landed(dw_parts.at[wrap(other - d, 4)], dw_recv.at[d])
    total = dw_parts[0].astype(F32)
    for i in range(1, 4):
        total += dw_parts[i].astype(F32)
    dw_total[...] = total.reshape(dw_total.shape)
    for d in range(8):
        there = lax.rem(z + d, 8)
        if d == 0:
            moves.local(dw_total.at[there], dw_z.at[z], dz_recv.at[d])
        else:
            moves.remote(dw_total.at[there], dw_z.at[z], dz_send.at[d], dz_recv.at[d], dw_mate(there))

    for d in range(16):
        for e in range(2):
            landed(d_relay.at[dp, core], a_recv.at[e, d])
    for d in range(16):
        there = lax.rem(dp + d, 16)
        d_pick[there] = d_relay[from_x[there], 0] + d_relay[from_x[there], 1]
        if d == 0:
            moves.local(d_pick.at[there], grad_lat.at[dp], b_recv.at[d])
        else:
            moves.remote(d_pick.at[there], grad_lat.at[dp], b_send.at[d], b_recv.at[d], (there, ctx))

    for d in range(8):
        landed(dw_z.at[wrap(z - d, 8)], dz_recv.at[d])
    total = dw_z[0]
    for i in range(1, 8):
        total += dw_z[i]
    for b in range(2):
        dw_last[b] = total[:, b * w_width:(b + 1) * w_width]
    odd = lax.rem(z, 2)

    def last_copy(b):
        return pltpu.make_async_remote_copy(
            src_ref=dw_last.at[b], dst_ref=grad_w.at[odd], send_sem=dl_send.at[b], recv_sem=dl_recv.at[odd],
            device_id=dw_home(b), device_id_type=MESH,
        )

    for b in range(2):
        @pl.when(is_me(dw_home(b)))
        def _():
            pltpu.make_async_copy(dw_last.at[b], grad_w.at[odd], dl_recv.at[odd]).start()

        @pl.when(jnp.logical_not(is_me(dw_home(b))))
        def _():
            last_copy(b).start()

    width = relay.shape[3]
    parts = []
    for d in range(15, -1, -1):
        source = wrap(dp - d, 16)
        landed(come.at[source], r_recv.at[d])
        sy, sx = source // 4, lax.rem(source, 4)
        for j, at in ((0, 8 * block_at(sx, z) + sy), (1, 8 * block_at(sy, z) + 4 + sx)):
            dst = grad_q.at[:, pl.ds(pl.multiple_of(at * width, width), width)]
            copy = pltpu.make_async_copy(come.at[source, j], dst, out_sem.at[d, j])
            copy.start()
            parts.append(copy)

    for d in range(16):
        landed(d_pick.at[dp], b_recv.at[d])
    for b in range(2):
        landed(dw_last.at[b], dl_recv.at[b])

        @pl.when(jnp.logical_not(is_me(dw_home(b))))
        def _():
            last_copy(b).wait_send()

        @pl.when(jnp.logical_not(w_here(b)))
        def _():
            w_copy(b).wait_send()

    for copy in moves.sent:
        copy.wait_send()

    def close(s, _):
        slot = slot_of(s)
        for k in range(1, 8):
            landed(gq.at[slot, 0, 0], gq_send.at[k, s])
        landed(d_halo.at[slot], z_send.at[1, s])

        @pl.when(s > 0)
        def _():
            landed(d_line.at[slot], d_send.at[s])

        return 0

    lax.fori_loop(0, 4, close, 0)
    for copy in parts:
        copy.wait()


def main_part(lo, from_x, from_y, q, latent, w, g):
    rows = q.shape[0]
    block, window = 2 * rows, 4 * rows
    q_width, g_width, w_width = q.shape[1] // 8, g.shape[1] // 8, 2 * w.shape[1]
    pairs = q_width // (2 * QK)
    quarter = LATENT // 4
    dma = pltpu.SemaphoreType.DMA
    vmem = pl.BlockSpec(memory_space=pltpu.VMEM)
    smem = pl.BlockSpec(memory_space=pltpu.SMEM)
    return pl.pallas_call(
        main_kernel,
        out_shape=[
            jax.ShapeDtypeStruct(q.shape, BF),
            jax.ShapeDtypeStruct((16, rows // 16, WIDE), F32),
            jax.ShapeDtypeStruct((2, LATENT // 32, w.shape[1]), F32),
        ],
        in_specs=[vmem, smem, smem] + [ANY] * 4,
        out_specs=[ANY] * 3,
        scratch_shapes=[
            pltpu.VMEM((4, 2, rows, q_width), BF),
            pltpu.VMEM((4, 2, rows, g_width), BF),
            pltpu.VMEM((4, 4, rows, WIDE), BF),
            pltpu.VMEM((4, quarter, w_width), BF),
            pltpu.VMEM((4, pairs, 2, rows, 2 * QK), BF),
            pltpu.VMEM((2, 16, rows, 2 * QK), BF),
            pltpu.VMEM((16, 2, rows, 2 * QK), BF),
            pltpu.VMEM((16, 2, rows, 2 * QK), BF),
            pltpu.VMEM((4, block, WIDE), BF),
            pltpu.VMEM((4, block, WIDE), BF),
            pltpu.VMEM((4, block, WIDE), F32),
            pltpu.VMEM((4, block, WIDE), BF),
            pltpu.VMEM((4, block, WIDE), BF),
            pltpu.VMEM((2, 16, rows // 16, WIDE), F32),
            pltpu.VMEM((16, 2, rows // 16, WIDE), F32),
            pltpu.VMEM((16, rows // 16, WIDE), F32),
            pltpu.VMEM((4, quarter, w_width), BF),
            pltpu.VMEM((4, quarter, w_width), BF),
            pltpu.VMEM((8, LATENT // 32, w_width), F32),
            pltpu.VMEM((8, LATENT // 32, w_width), F32),
            pltpu.VMEM((2, LATENT // 32, w.shape[1]), F32),
            pltpu.VMEM((window, w_width), BF),
            pltpu.VMEM((window, w_width), BF),
            pltpu.VMEM((2, window, block), BF),
            pltpu.VMEM((2, window, block), BF),
            pltpu.VMEM((LATENT, w_width), F32),
            pltpu.VMEM((window, ROPE), F32),
            dma((3, 8)), dma((3, 8)), dma((2,)), dma((2,)), dma((4,)), dma((4,)), dma((2, 4)), dma((2, 4)),
            dma((8, 4)), dma((8, 4)), dma((4,)), dma((4,)),
            dma((2, 16)), dma((2, 16)), dma((16,)), dma((16,)), dma((16,)), dma((16,)), dma((16, 2)),
            dma((4,)), dma((4,)), dma((8,)), dma((8,)), dma((2,)), dma((2,)),
        ],
        compiler_params=pltpu.CompilerParams(
            collective_id=0, has_side_effects=True, vmem_limit_bytes=60 * 1024 * 1024
        ),
        name="heads_and_exchanges",
    )(lo, from_x, from_y, q, latent, w, g)


def body(queries, latent, w_kv, grad_out, doc_lengths, matching):
    y, x, z, core = place()
    dp = 4 * y + x
    rows = queries.shape[0]
    block = 2 * rows

    packs = pick(core, 4 * y + jnp.arange(4), 4 * jnp.arange(4) + x)
    ends = jnp.cumsum(doc_lengths[packs], axis=1)
    token = z * block + jnp.arange(block, dtype=jnp.int32)
    begun = jnp.where(ends[:, None, :] <= token[None, :, None], ends[:, None, :], 0)
    lo = (jnp.max(begun, axis=2) - (z - 1) * block)[:, None, :].astype(jnp.int32)

    turned = 4 * lax.rem(matching, 4) + matching // 4
    grad_queries, grad_latent, grad_weight = main_part(lo, matching, turned, queries, latent, w_kv, grad_out)
    return grad_queries, grad_latent.reshape(rows, WIDE), grad_weight.reshape(LATENT // 16, -1)


def solution(mesh):
    in_specs = (
        P(("dp", "ctx"), None),
        P(("dp", "ctx"), None),
        P(None, "ctx"),
        P(("dp", "ctx"), None),
        P(),
        P(),
    )
    out_specs = (P(("dp", "ctx"), None), P(("dp", "ctx"), None), P("dp", "ctx"))
    return jax.shard_map(body, mesh=mesh, in_specs=in_specs, out_specs=out_specs, check_vma=False)
```

time: 248 us -> 210 us (0.85)
  starting transfers between devices: 12 us -> 0 us
  Pallas kernels: 204 us -> 197 us
  other arithmetic: 8.07 us -> 1.49 us
  waiting for transfers between devices: 6.32 us -> 0 us
  local copies, waits for them, and re-layouts: 14.2 us -> 9.24 us
    all_to_all x1 -> x0, starting transfers between devices: 10 us -> none  [body(): lax.all_to_all(lat_chosen, 'dp', split_axis=0, concat_axis=0, tiled=True)]
    pallas_call x2 -> x1, Pallas kernels: 204 us -> 197 us  [main_part(): pl.pallas_call(main_kernel, out_shape=[jax.ShapeDtypeStruct(q.shape, BF),...]
    all_to_all x1 -> x0, waiting for transfers between devices: 6.31 us -> none  [body(): lax.all_to_all(lat_chosen, 'dp', split_axis=0, concat_axis=0, tiled=True)]
    gather x3 -> x0, local copies, waits for them, and re-layouts: 5.14 us -> none  [the longest x2 3.85 us: body(): chosen = jnp.stack([relay[0][major, minor], relay[1][minor, major]], axis=1)]
    another operation x1 -> x0, other arithmetic: 3.42 us -> none  [body(): chosen = jnp.stack([relay[0][major, minor], relay[1][minor, major]], axis=1)]
    reduce_sum x2 -> x0, other arithmetic: 2.62 us -> none  [the longest x1 1.32 us: body(): lat_chosen = jnp.sum(lat_relay, axis=1)[matching]]
    unnamed x12 -> x8, local copies, waits for them, and re-layouts: 5.53 us -> 8.08 us
  transfers between devices with their start and end apart: 3 -> 0, of which waited for: 1 -> 0; matrix products, arithmetic and copies ran while one was open for 2% -> 0% of each run, Pallas kernels for 0% -> 0%
where the time goes in v3:
time: 210 us; the launch traced here: 208 us
  Pallas kernels  197 us (94%)
  local copies, waits for them, and re-layouts  9.24 us (4%)
    pallas_call x1, Pallas kernels, main_part(): pl.pallas_call(main_kernel, out_shape=[jax.ShapeDtypeStruct(q.shape, BF),...  197 us
    unnamed x8, local copies, waits for them, and re-layouts  8.08 us

profile of v3, /device:TPU:1, one launch (start us, length us, event | category | flops | bytes accessed | tf_op | source)
XLA Modules:
  0.0 208.3 jit_solution(3361955560131949635)
XLA Ops:
  0.6 0.0 copy-start
  0.7 1.2 multiply_add_fusion.from_y
  1.9 0.0 copy-done
  1.9 0.6 gather_fusion
  2.4 0.2 reduce_window_sum.11
  2.6 0.1 select_reduce_fusion
  2.8 0.6 sub.39.lo
  3.4 1.7 copy.11.latent
  5.1 196.8 %heads_and_exchanges.1 = (bf16[128,12288]{1,0:T(8,128)(2,1)}, f32[16,8,576]{2,1,0:T(8,128)}, f32[2,16,1024]{2,1,0:T(8,128)}) custom-call(s32[4,1,256]{2,1,0:T(1,128)} %sub.39.lo, s32[16]{0:T(128)} %from_x.1, s32[16]{0:T(128)} %multiply_add_fusion.from_y, bf16[128,12288]{1,0:T(8,128)(2,1)} %q.1, bf16[128,576]{1,0:T(8,128)(2,1)} %copy.11.latent, ...), custom_call_target="tpu_custom_call" | custom-call | tf_op jit(solution)/shard_map/heads_and_exchanges/pallas_call | solution.py:530
  201.9 1.8 copy.12
  203.7 0.0 copy-start.1
  203.7 3.9 %copy.15 = bf16[128,12288]{1,0:T(8,128)(2,1)} copy(bf16[128,12288]{1,0:T(8,128)(2,1)} %get-tuple-element.18) | data formatting | bytes 6291456
  207.6 0.0 copy-done.1
  207.6 0.7 copy.16
  (4 shorter events, 0.0 us)
Async XLA Ops:
  0.6 1.2 copy-start
  203.7 3.9 %copy-start.1 = (f32[2,16,1024]{2,1,0:T(8,128)S(1)}, f32[2,16,1024]{2,1,0:T(8,128)}, u32[]{:S(2)}) copy-start(f32[2,16,1024]{2,1,0:T(8,128)} %get-tuple-element.8) | copy-start | bytes 393220

commit v4 on v3

v4 whole, which is shorter than its diff:
```python
import jax
import jax.numpy as jnp
from jax import lax
from jax.experimental import pallas as pl
from jax.experimental.pallas import tpu as pltpu
from jax.sharding import PartitionSpec as P

NOPE = 128
ROPE = 64
VDIM = 128
LATENT = 512
HEADS = 64
ROWS = 128
QK = NOPE + ROPE
KV = NOPE + VDIM
WIDE = LATENT + ROPE
MESH = pl.DeviceIdType.MESH
ANY = pl.BlockSpec(memory_space=pl.ANY)
BF = jnp.bfloat16
F32 = jnp.float32
LOW = -1e30


def place():
    dp, ctx = lax.axis_index("dp"), lax.axis_index("ctx")
    return dp // 4, lax.rem(dp, 4), ctx // 2, lax.rem(ctx, 2)


def pick(axis, on_x, on_y):
    return (1 - axis) * on_x + axis * on_y


def wrap(value, n):
    return lax.rem(value + n, n)


def line_dp(axis, position, y, x):
    return pick(axis, 4 * y + position, 4 * position + x)


class Sender:
    def __init__(self):
        self.sent = []
        self.due = []

    def remote(self, src, dst, send_sem, recv_sem, device):
        copy = pltpu.make_async_remote_copy(
            src_ref=src, dst_ref=dst, send_sem=send_sem, recv_sem=recv_sem,
            device_id=device, device_id_type=MESH,
        )
        copy.start()
        self.sent.append(copy)
        return copy

    def local(self, src, dst, sem):
        copy = pltpu.make_async_copy(src, dst, sem)
        copy.start()
        self.due.append(copy)


def signal(device):
    pl.semaphore_signal(pltpu.get_barrier_semaphore(), inc=1, device_id=device, device_id_type=MESH)


def block_at(position, z):
    return lax.rem(position + 8 - z, 4)


def landed(ref, sem):
    pltpu.make_async_copy(ref, ref, sem).wait()


def nt(a, b):
    return lax.dot_general(a, b, (((1,), (1,)), ((), ())), preferred_element_type=F32)


def tn(a, b):
    return lax.dot_general(a, b, (((0,), (0,)), ((), ())), preferred_element_type=F32)


def nn(a, b):
    return jnp.dot(a, b, preferred_element_type=F32)


def heads(t, pair, lo, q, g, lat, w, gq, d_acc, dw_acc, p_t, ds_t):
    rows = q.shape[3]
    block = 2 * rows
    window = 4 * rows
    scale = float(QK) ** -0.5

    nope = lat[t, :, :, :LATENT].reshape(window, LATENT)
    rope = lat[t, :, :, LATENT:].reshape(window, ROPE)
    w_two = w[pair].reshape(LATENT, 2 * KV)
    lows = lo[t]
    key_at = lax.broadcasted_iota(jnp.int32, (3 * rows, rows), 0)
    query_at = lax.broadcasted_iota(jnp.int32, (3 * rows, rows), 1)
    kv_two = nn(nope, w_two).astype(BF)
    q_two = q[pair, t].reshape(block, 2 * QK)
    g_two = g[pair, t].reshape(block, 2 * VDIM)
    dq_two, dkv_two = [], []
    d_rope = None
    for h in range(2):
        qh = q_two[:, h * QK:(h + 1) * QK]
        gh = g_two[:, h * VDIM:(h + 1) * VDIM]
        kh = jnp.concatenate([kv_two[:, h * KV:h * KV + NOPE], rope], axis=1)
        vh = kv_two[:, h * KV + NOPE:(h + 1) * KV]
        scores = nt(kh, qh)
        dprobs = nt(vh, gh)
        for s in range(2):
            keys = slice(rows * s, rows * s + 3 * rows)
            queries = slice(rows * s, rows * s + rows)
            low = lows[:, queries] - rows * s
            seen = (key_at >= low) & (key_at <= query_at + block)
            sc = jnp.where(seen, scores[keys, queries] * scale, LOW)
            top = jnp.max(sc, axis=0, keepdims=True)
            ex = jnp.exp(sc - top)
            probs = ex * (1.0 / jnp.sum(ex, axis=0, keepdims=True))
            probs_low = probs.astype(BF)
            dp = dprobs[keys, queries]
            row_dot = jnp.sum(probs_low.astype(F32) * dp, axis=0, keepdims=True)
            p_t[h, keys, queries] = probs_low
            ds_t[h, keys, queries] = (probs * (dp - row_dot)).astype(BF)
        ds = ds_t[h]
        dq_two.append((tn(ds, kh) * scale).astype(BF))
        dk = nn(ds, qh) * scale
        dv = nn(p_t[h], gh)
        d_rope = dk[:, NOPE:] if d_rope is None else d_rope + dk[:, NOPE:]
        dkv_two += [dk[:, :NOPE].astype(BF), dv.astype(BF)]
    gkv = jnp.concatenate(dkv_two, axis=1)
    gq[pair, t] = jnp.concatenate(dq_two, axis=1).reshape(2, rows, 2 * QK)
    d_acc[t, :, :LATENT] += nt(gkv, w_two)
    d_acc[t, :, LATENT:] += d_rope
    dw_acc[...] += tn(nope, gkv)


def main_kernel(
    lo, from_x, from_y, q, latent, w, g,
    grad_q, grad_lat, grad_w,
    q_all, g_all, lat_all, w_all, gq, relay, relay_now, chosen, come,
    d_acc, d_halo, d_in, d_line, d_lat, d_sum, d_cross, d_relay, d_pick,
    dw, dw_parts, dw_total, dw_z, dw_last, dw_acc, p_t, ds_t,
    send, recv, l_send, l_recv, w_send, w_recv, w_send2, w_recv2, z_send, z_recv, gq_send, gq_recv,
    d_send, d_recv, c_send, c_recv, a_send, a_recv, b_send, b_recv, r_send, r_recv, out_sem,
    dw_send, dw_recv, dz_send, dz_recv, dl_send, dl_recv,
):
    y, x, z, core = place()
    dp = 4 * y + x
    ctx = 2 * z + core
    mine = pick(core, x, y)
    other = pick(core, y, x)
    before, after = wrap(z - 1, 8), wrap(z + 1, 8)
    rows = q.shape[0]
    block = 2 * rows
    quarter = LATENT // 4
    piece = rows // 4
    two_kv = 2 * KV
    two_q = 2 * QK
    two_v = 2 * VDIM

    w_axis = lax.rem(z, 2)
    w_first = lax.rem(pick(w_axis, x, y) + 4 - z // 2, 4)
    w_other = pick(w_axis, y, x)
    part = block_at(mine, z)
    w_plane = 2 * part + core

    def dw_mate(plane):
        return line_dp(core, lax.rem(part + plane, 4), y, x), 2 * plane + core

    def dw_home(b):
        return 4 * other + z // 2, 2 * w_plane + b

    def dw_source(odd):
        plane = 2 * x + odd
        spot = lax.rem(z // 2 + plane, 4)
        return pick(w_axis, 4 * y + spot, 4 * spot + y), 2 * plane + w_axis

    def is_me(device):
        return (device[0] == dp) & (device[1] == ctx)

    def not_me(device):
        return jnp.logical_not(is_me(device))

    for d in range(16):
        there = lax.rem(dp + d, 16)
        if d:
            signal((there, ctx))
        signal((there, 2 * z + 1 - core))
    signal((dp, 2 * before + core))
    signal((dp, 2 * after + core))
    for d in range(1, 8):
        signal(dw_mate(lax.rem(z + d, 8)))
    strangers = 0
    for b in range(2):
        @pl.when(not_me((dp, 2 * w_plane + b)))
        def _():
            signal((dp, 2 * w_plane + b))

        @pl.when(not_me(dw_source(b)))
        def _():
            signal(dw_source(b))

        strangers += jnp.where(is_me((dp, 2 * (w_first + 4 * b) + w_axis)), 0, 1)
        strangers += jnp.where(is_me(dw_home(b)), 0, 1)

    pl.semaphore_wait(pltpu.get_barrier_semaphore(), 31 + 2 + 7 + strangers)

    moves = Sender()

    def w_home(i):
        return dp, 2 * (w_first + 4 * i) + w_axis

    def w_ends(k):
        src = w.at[pl.ds(pl.multiple_of(w_other * quarter, quarter), quarter), pl.ds(k * two_kv, two_kv)]
        return src, w_all.at[2 * core + k, w_other]

    def w_copy(k, i):
        src, dst = w_ends(k)
        return pltpu.make_async_remote_copy(
            src_ref=src, dst_ref=dst, send_sem=w_send.at[k, i], recv_sem=w_recv.at[2 * core + k],
            device_id=w_home(i), device_id_type=MESH,
        )

    def send_w(k):
        for i in range(2):
            @pl.when(is_me(w_home(i)))
            def _():
                src, dst = w_ends(k)
                pltpu.make_async_copy(src, dst, w_recv.at[2 * core + k]).start()

            @pl.when(not_me(w_home(i)))
            def _():
                w_copy(k, i).start()

    def share_w(pair):
        landed(w_all.at[pair, other], w_recv.at[pair])
        for d in range(1, 4):
            target = (line_dp(1 - core, lax.rem(other + d, 4), y, x), 2 * z + core)
            moves.remote(
                w_all.at[pair, other], w_all.at[pair, other], w_send2.at[pair, d], w_recv2.at[pair, d], target
            )

    def send_latent(d, e):
        axis = lax.rem(core + e, 2)
        spot = pick(axis, x, y)
        k = 4 * e + d
        dst = lat_all.at[spot, 2 + core]
        if d == 0 and e == 0:
            moves.local(latent, dst, l_recv.at[k])
        else:
            target = (line_dp(axis, lax.rem(spot + d, 4), y, x), 2 * z + axis)
            moves.remote(latent, dst, l_send.at[k], l_recv.at[k], target)

    def send_rows(pair, d, e):
        axis = lax.rem(core + e, 2)
        spot = pick(axis, x, y)
        there = lax.rem(spot + d, 4)
        target = (line_dp(axis, there, y, x), 2 * z + axis)
        k = 4 * e + d
        at = 4 * (2 * block_at(there, z) + axis) + pair
        q_part = q.at[:, pl.ds(pl.multiple_of(at * two_q, two_q), two_q)]
        g_part = g.at[:, pl.ds(pl.multiple_of(at * two_v, two_v), two_v)]
        q_dst, g_dst = q_all.at[pair, spot, core], g_all.at[pair, spot, core]
        if d == 0 and e == 0:
            moves.local(q_part, q_dst, recv.at[0, pair, k])
            moves.local(g_part, g_dst, recv.at[1, pair, k])
        else:
            moves.remote(q_part, q_dst, send.at[0, pair, k], recv.at[0, pair, k], target)
            moves.remote(g_part, g_dst, send.at[1, pair, k], recv.at[1, pair, k], target)

    def forward_latent(d):
        slot = wrap(mine - d, 4)
        for e in range(2):
            landed(lat_all.at[slot, 2 + lax.rem(core + e, 2)], l_recv.at[4 * e + d])
        moves.remote(
            lat_all.at[slot, pl.ds(2, 2)], lat_all.at[slot, pl.ds(0, 2)],
            z_send.at[0, d], z_recv.at[0, d], (dp, 2 * after + core),
        )

    send_w(0)
    for d in (0, 1, 3, 2):
        for e in range(2):
            send_latent(d, e)
    send_w(1)
    for d in (0, 1, 3, 2):
        for e in range(2):
            send_rows(0, d, e)
    d_acc[...] = jnp.zeros_like(d_acc)
    forward_latent(0)
    share_w(0)
    forward_latent(1)
    share_w(2)
    forward_latent(3)
    forward_latent(2)
    for d in (0, 1, 3, 2):
        for e in range(2):
            send_rows(2, d, e)
    share_w(1)
    share_w(3)
    for pair in (1, 3):
        for d in (0, 1, 3, 2):
            for e in range(2):
                send_rows(pair, d, e)
    p_t[...] = jnp.zeros_like(p_t)
    ds_t[...] = jnp.zeros_like(ds_t)

    def order(s):
        return s + (s // 2) * (1 - 2 * lax.rem(s, 2))

    def slot_of(s):
        return lax.rem(mine + 4 - order(s), 4)

    def pair_of(i):
        return 2 * lax.rem(i, 2) + i // 2

    def gq_copy(i, there, e, d, half):
        return pltpu.make_async_remote_copy(
            src_ref=gq.at[pair_of(i), :, half, pl.ds(pl.multiple_of(there * piece, piece), piece)],
            dst_ref=relay.at[i, core, pl.ds(4 * other, 4)],
            send_sem=gq_send.at[4 * e + d, i], recv_sem=gq_recv.at[4 * e + d, i],
            device_id=(line_dp(1 - core, there, y, x), 2 * z + half), device_id_type=MESH,
        )

    def relay_pair(i):
        for dm in (2, 1, 3, 0):
            there = lax.rem(other + dm, 4)
            for e in range(2):
                half = lax.rem(core + e, 2)
                if dm == 0 and e == 0:
                    src = gq.at[pair_of(i), :, half, pl.ds(pl.multiple_of(there * piece, piece), piece)]
                    pltpu.make_async_copy(src, relay.at[i, core, pl.ds(4 * other, 4)], gq_recv.at[0, i]).start()
                else:
                    gq_copy(i, there, e, dm, half).start()

    def r_copy(i, d):
        there = lax.rem(dp + d, 16)
        return pltpu.make_async_remote_copy(
            src_ref=chosen.at[i, there], dst_ref=come.at[i, dp], send_sem=r_send.at[i, d], recv_sem=r_recv.at[i, d],
            device_id=(there, ctx), device_id_type=MESH,
        )

    def deliver(i):
        for k in range(8):
            landed(relay.at[i, core, pl.ds(4 * other, 4)], gq_recv.at[k, i])
        relay_now[...] = relay[i]
        for d in (10, 2, 8, 6, 14, 9, 11, 1, 3, 4, 12, 5, 15, 7, 13, 0):
            there = lax.rem(dp + d, 16)
            chosen[i, there, 0] = relay_now[0, from_x[there]]
            chosen[i, there, 1] = relay_now[1, from_y[there]]
            if d == 0:
                pltpu.make_async_copy(chosen.at[i, there], come.at[i, dp], r_recv.at[i, d]).start()
            else:
                r_copy(i, d).start()

    def dw_copy(i, d):
        there = lax.rem(other + d, 4)
        return pltpu.make_async_remote_copy(
            src_ref=dw.at[i, there], dst_ref=dw_parts.at[i, other], send_sem=dw_send.at[i, d],
            recv_sem=dw_recv.at[i, d], device_id=(line_dp(1 - core, there, y, x), 2 * z + core), device_id_type=MESH,
        )

    def weight_first(i):
        dw[i] = dw_acc[...].astype(BF).reshape(4, quarter, two_kv)
        for d in (2, 1, 3, 0):
            if d == 0:
                pltpu.make_async_copy(dw.at[i, other], dw_parts.at[i, other], dw_recv.at[i, d]).start()
            else:
                dw_copy(i, d).start()

    def dz_copy(i, d):
        there = lax.rem(z + d, 8)
        return pltpu.make_async_remote_copy(
            src_ref=dw_total.at[i, there], dst_ref=dw_z.at[i, z], send_sem=dz_send.at[i, d],
            recv_sem=dz_recv.at[i, d], device_id=dw_mate(there), device_id_type=MESH,
        )

    def weight_second(i):
        for d in range(4):
            landed(dw_parts.at[i, wrap(other - d, 4)], dw_recv.at[i, d])
        total = dw_parts[i, 0].astype(F32)
        for n in range(1, 4):
            total += dw_parts[i, n].astype(F32)
        dw_total[i] = total.astype(BF).reshape(8, quarter // 8, two_kv)
        for d in (4, 3, 5, 2, 6, 1, 7, 0):
            if d == 0:
                pltpu.make_async_copy(dw_total.at[i, z], dw_z.at[i, z], dz_recv.at[i, d]).start()
            else:
                dz_copy(i, d).start()

    odd = lax.rem(z, 2)

    def last_ends(i):
        pair = pair_of(i)
        k = lax.rem(pair, 2)
        return dw_last.at[i], grad_w.at[odd, k], dl_recv.at[odd, k], dw_home(pair // 2)

    def last_copy(i):
        src, dst, sem, home = last_ends(i)
        return pltpu.make_async_remote_copy(
            src_ref=src, dst_ref=dst, send_sem=dl_send.at[i], recv_sem=sem, device_id=home, device_id_type=MESH
        )

    def weight_third(i):
        for d in range(8):
            landed(dw_z.at[i, wrap(z - d, 8)], dz_recv.at[i, d])
        total = dw_z[i, 0].astype(F32)
        for n in range(1, 8):
            total += dw_z[i, n].astype(F32)
        dw_last[i] = total
        src, dst, sem, home = last_ends(i)

        @pl.when(is_me(home))
        def _():
            pltpu.make_async_copy(src, dst, sem).start()

        @pl.when(not_me(home))
        def _():
            last_copy(i).start()

    def halo_copy(s, slot):
        return pltpu.make_async_remote_copy(
            src_ref=d_halo.at[slot], dst_ref=d_in.at[slot], send_sem=z_send.at[1, s], recv_sem=z_recv.at[1, s],
            device_id=(dp, 2 * before + core), device_id_type=MESH,
        )

    def d_copy(s, slot):
        return pltpu.make_async_remote_copy(
            src_ref=d_line.at[slot], dst_ref=d_lat.at[mine], send_sem=d_send.at[s], recv_sem=d_recv.at[s],
            device_id=(line_dp(core, slot, y, x), 2 * z + core), device_id_type=MESH,
        )

    def add_halo(s):
        slot = slot_of(s)
        landed(d_in.at[slot], z_recv.at[1, s])
        d_line[slot] = (d_acc[slot, block:] + d_in[slot].astype(F32)).astype(BF)

        @pl.when(s == 0)
        def _():
            pltpu.make_async_copy(d_line.at[slot], d_lat.at[mine], d_recv.at[s]).start()

        @pl.when(s > 0)
        def _():
            d_copy(s, slot).start()

    def step(n, _):
        i, s = n // 4, lax.rem(n, 4)
        pair = pair_of(i)
        d = order(s)
        slot = slot_of(s)

        @pl.when(s == 0)
        def _():
            dw_acc[...] = jnp.zeros_like(dw_acc)
            for dm in range(1, 4):
                landed(w_all.at[pair, wrap(other - dm, 4)], w_recv2.at[pair, dm])

        @pl.when(i == 0)
        def _():
            landed(lat_all.at[slot, pl.ds(0, 2)], z_recv.at[0, d])

        for e in range(2):
            half = lax.rem(core + e, 2)
            landed(q_all.at[pair, slot, half], recv.at[0, pair, 4 * e + d])
            landed(g_all.at[pair, slot, half], recv.at[1, pair, 4 * e + d])
        heads(slot, pair, lo, q_all, g_all, lat_all, w_all, gq, d_acc, dw_acc, p_t, ds_t)

        @pl.when(i == 3)
        def _():
            d_halo[slot] = d_acc[slot, :block].astype(BF)
            halo_copy(s, slot).start()

            @pl.when(s > 0)
            def _():
                add_halo(s - 1)

        @pl.when(s == 3)
        def _():
            relay_pair(i)
            weight_first(i)

        @pl.when((s == 2) & (i > 0))
        def _():
            deliver(i - 1)
            weight_second(i - 1)

        @pl.when((s == 2) & (i > 1))
        def _():
            weight_third(i - 2)

        return 0

    lax.fori_loop(0, 16, step, 0)

    three = jnp.int32(3)
    add_halo(three)
    deliver(three)
    weight_second(three)

    def collect(s, _):
        landed(d_lat.at[lax.rem(mine + order(s), 4)], d_recv.at[s])
        return 0

    lax.fori_loop(0, 4, collect, 0)
    total = d_lat[0].astype(F32)
    for i in range(1, 4):
        total += d_lat[i].astype(F32)
    d_sum[...] = total.reshape(d_sum.shape)
    moves.remote(d_sum.at[1 - core], d_cross, c_send, c_recv, (dp, 2 * z + 1 - core))
    weight_third(jnp.int32(2))
    landed(d_cross, c_recv)
    d_sum[core] += d_cross[...]
    for d in range(16):
        there = lax.rem(dp + d, 16)
        if d == 0:
            moves.local(d_sum.at[core, there], d_relay.at[dp], a_recv.at[d])
        else:
            moves.remote(d_sum.at[core, there], d_relay.at[dp], a_send.at[d], a_recv.at[d], (there, ctx))

    def put(i):
        for d in range(15, -1, -1):
            source = wrap(dp - d, 16)
            landed(come.at[i, source], r_recv.at[i, d])
            sy, sx = source // 4, lax.rem(source, 4)
            for j, at, row in ((0, 8 * block_at(sx, z), sy), (1, 8 * block_at(sy, z) + 4, sx)):
                dst = grad_q.at[
                    pl.ds(pl.multiple_of(row * piece, piece), piece),
                    pl.ds(pl.multiple_of((at + pair_of(i)) * two_q, two_q), two_q),
                ]
                pltpu.make_async_copy(come.at[i, source, j], dst, out_sem).start()

    def put_early(i, _):
        put(i)
        return 0

    lax.fori_loop(0, 3, put_early, 0)
    for d in range(16):
        landed(d_relay.at[dp], a_recv.at[d])
    for d in range(16):
        there = lax.rem(dp + d, 16)
        d_pick[there] = d_relay[from_x[there]]
        if d == 0:
            moves.local(d_pick.at[there], grad_lat.at[dp], b_recv.at[d])
        else:
            moves.remote(d_pick.at[there], grad_lat.at[dp], b_send.at[d], b_recv.at[d], (there, ctx))
    weight_third(three)
    put(three)

    for d in range(16):
        landed(d_pick.at[dp], b_recv.at[d])
    for b in range(2):
        for k in range(2):
            landed(dw_last.at[0], dl_recv.at[b, k])

            @pl.when(not_me(w_home(b)))
            def _():
                w_copy(k, b).wait_send()

    for copy in moves.sent:
        copy.wait_send()

    def close(i, _):
        for k in range(1, 8):
            landed(relay.at[i, core, pl.ds(4 * other, 4)], gq_send.at[k, i])
        for d in range(1, 16):
            r_copy(i, d).wait_send()
        for d in range(1, 4):
            dw_copy(i, d).wait_send()
        for d in range(1, 8):
            dz_copy(i, d).wait_send()

        @pl.when(not_me(dw_home(pair_of(i) // 2)))
        def _():
            last_copy(i).wait_send()

        slot = slot_of(i)
        landed(d_halo.at[slot], z_send.at[1, i])

        @pl.when(i > 0)
        def _():
            landed(d_line.at[slot], d_send.at[i])

        return 0

    lax.fori_loop(0, 4, close, 0)
    landed(grad_q, out_sem)


def main_part(lo, from_x, from_y, q, latent, w, g):
    rows = q.shape[0]
    block, window = 2 * rows, 4 * rows
    quarter = LATENT // 4
    two_q, two_v, two_kv = 2 * QK, 2 * VDIM, 2 * KV
    dma = pltpu.SemaphoreType.DMA
    vmem = pl.BlockSpec(memory_space=pltpu.VMEM)
    smem = pl.BlockSpec(memory_space=pltpu.SMEM)
    return pl.pallas_call(
        main_kernel,
        out_shape=[
            jax.ShapeDtypeStruct(q.shape, BF),
            jax.ShapeDtypeStruct((16, rows // 16, WIDE), F32),
            jax.ShapeDtypeStruct((2, 2, quarter // 8, two_kv), F32),
        ],
        in_specs=[vmem, smem, smem] + [ANY] * 4,
        out_specs=[ANY] * 3,
        scratch_shapes=[
            pltpu.VMEM((4, 4, 2, rows, two_q), BF),
            pltpu.VMEM((4, 4, 2, rows, two_v), BF),
            pltpu.VMEM((4, 4, rows, WIDE), BF),
            pltpu.VMEM((4, 4, quarter, two_kv), BF),
            pltpu.VMEM((4, 4, 2, rows, two_q), BF),
            pltpu.VMEM((4, 2, 16, rows // 4, two_q), BF),
            pltpu.VMEM((2, 16, rows // 4, two_q), BF),
            pltpu.VMEM((4, 16, 2, rows // 4, two_q), BF),
            pltpu.VMEM((4, 16, 2, rows // 4, two_q), BF),
            pltpu.VMEM((4, window, WIDE), F32),
            pltpu.VMEM((4, block, WIDE), BF),
            pltpu.VMEM((4, block, WIDE), BF),
            pltpu.VMEM((4, block, WIDE), BF),
            pltpu.VMEM((4, block, WIDE), BF),
            pltpu.VMEM((2, 16, rows // 16, WIDE), F32),
            pltpu.VMEM((16, rows // 16, WIDE), F32),
            pltpu.VMEM((16, rows // 16, WIDE), F32),
            pltpu.VMEM((16, rows // 16, WIDE), F32),
            pltpu.VMEM((4, 4, quarter, two_kv), BF),
            pltpu.VMEM((4, 4, quarter, two_kv), BF),
            pltpu.VMEM((4, 8, quarter // 8, two_kv), BF),
            pltpu.VMEM((4, 8, quarter // 8, two_kv), BF),
            pltpu.VMEM((4, quarter // 8, two_kv), F32),
            pltpu.VMEM((LATENT, two_kv), F32),
            pltpu.VMEM((2, window, block), BF),
            pltpu.VMEM((2, window, block), BF),
            dma((2, 4, 8)), dma((2, 4, 8)), dma((8,)), dma((8,)), dma((2, 2)), dma((4,)), dma((4, 4)), dma((4, 4)),
            dma((2, 4)), dma((2, 4)), dma((8, 4)), dma((8, 4)), dma((4,)), dma((4,)), dma, dma,
            dma((16,)), dma((16,)), dma((16,)), dma((16,)), dma((4, 16)), dma((4, 16)), dma,
            dma((4, 4)), dma((4, 4)), dma((4, 8)), dma((4, 8)), dma((4,)), dma((2, 2)),
        ],
        compiler_params=pltpu.CompilerParams(
            collective_id=0, has_side_effects=True, vmem_limit_bytes=60 * 1024 * 1024
        ),
        name="heads_and_exchanges",
    )(lo, from_x, from_y, q, latent, w, g)


def body(queries, latent, w_kv, grad_out, doc_lengths, matching):
    y, x, z, core = place()
    dp = 4 * y + x
    rows = queries.shape[0]
    block = 2 * rows

    packs = pick(core, 4 * y + jnp.arange(4), 4 * jnp.arange(4) + x)
    ends = jnp.cumsum(doc_lengths[packs], axis=1)
    token = z * block + jnp.arange(block, dtype=jnp.int32)
    begun = jnp.where(ends[:, None, :] <= token[None, :, None], ends[:, None, :], 0)
    lo = (jnp.max(begun, axis=2) - (z - 1) * block)[:, None, :].astype(jnp.int32)

    turned = 4 * lax.rem(matching, 4) + matching // 4
    grad_queries, grad_latent, grad_weight = main_part(lo, matching, turned, queries, latent, w_kv, grad_out)
    return grad_queries, grad_latent.reshape(rows, WIDE), grad_weight.transpose(0, 2, 1, 3).reshape(LATENT // 16, -1)


def solution(mesh):
    in_specs = (
        P(("dp", "ctx"), None),
        P(("dp", "ctx"), None),
        P(None, "ctx"),
        P(("dp", "ctx"), None),
        P(),
        P(),
    )
    out_specs = (P(("dp", "ctx"), None), P(("dp", "ctx"), None), P("dp", "ctx"))
    return jax.shard_map(body, mesh=mesh, in_specs=in_specs, out_specs=out_specs, check_vma=False)
```

time: 210 us -> 186 us (0.89)
  the two profiles are of different devices: /device:TPU:1 before, /device:TPU:33 now
where the time goes in v4:
time: 186 us
  Pallas kernels  174 us (94%)
  local copies, waits for them, and re-layouts  10.2 us (5%)
    pallas_call x1, Pallas kernels, main_part(): pl.pallas_call(main_kernel, out_shape=[jax.ShapeDtypeStruct(q.shape, BF),...  174 us
    unnamed x6, local copies, waits for them, and re-layouts  8.07 us

profile of v4, /device:TPU:33, one launch (start us, length us, event | category | flops | bytes accessed | tf_op | source)
XLA Modules:
  0.0 186.1 jit_solution(17545786252043497642)
XLA Ops:
  0.6 0.0 copy-start
  0.7 1.2 multiply_add_fusion.from_y
  1.9 0.0 copy-done
  1.9 0.6 gather_fusion
  2.4 0.2 reduce_window_sum.11
  2.6 0.1 select_reduce_fusion
  2.8 0.6 sub.39.lo
  3.4 1.7 copy.14.latent
  5.1 173.7 %heads_and_exchanges.1 = (bf16[128,12288]{1,0:T(8,128)(2,1)}, f32[16,8,576]{2,1,0:T(8,128)}, f32[2,2,16,512]{3,2,1,0:T(8,128)}) custom-call(s32[4,1,256]{2,1,0:T(1,128)} %sub.39.lo, s32[16]{0:T(128)} %from_x.1, s32[16]{0:T(128)} %multiply_add_fusion.from_y, bf16[128,12288]{1,0:T(8,128)(2,1)} %q.1, bf16[128,576]{1,0:T(8,128)(2,1)} %copy.14.latent, ...), custom_call_target="tpu_custom_call" | custom-call | tf_op jit(solution)/shard_map/heads_and_exchanges/pallas_call | solution.py:595
  178.8 1.8 copy.16
  180.6 1.0 copy.15
  181.6 0.7 copy.17
  182.3 3.8 %copy.19 = bf16[128,12288]{1,0:T(8,128)(2,1)} copy(bf16[128,12288]{1,0:T(8,128)(2,1)} %get-tuple-element.21) | data formatting | bytes 6291456
  (4 shorter events, 0.0 us)
Async XLA Ops:
  0.6 1.2 copy-start

commit v5 on v4

--- a/solution.py
+++ b/solution.py
@@ -90,7 +90,7 @@
 
     nope = lat[t, :, :, :LATENT].reshape(window, LATENT)
     rope = lat[t, :, :, LATENT:].reshape(window, ROPE)
-    w_two = w[pair].reshape(LATENT, 2 * KV)
+    w_two = w[pair]
     lows = lo[t]
     key_at = lax.broadcasted_iota(jnp.int32, (3 * rows, rows), 0)
     query_at = lax.broadcasted_iota(jnp.int32, (3 * rows, rows), 1)
@@ -134,9 +134,9 @@
 
 
 def main_kernel(
-    lo, from_x, from_y, q, latent, w, g,
+    lengths, matching, q, latent, w, g,
     grad_q, grad_lat, grad_w,
-    q_all, g_all, lat_all, w_all, gq, relay, relay_now, chosen, come,
+    lo, q_all, g_all, lat_all, w_all, gq, relay, relay_now, chosen, come,
     d_acc, d_halo, d_in, d_line, d_lat, d_sum, d_cross, d_relay, d_pick,
     dw, dw_parts, dw_total, dw_z, dw_last, dw_acc, p_t, ds_t,
     send, recv, l_send, l_recv, w_send, w_recv, w_send2, w_recv2, z_send, z_recv, gq_send, gq_recv,
@@ -209,9 +209,12 @@
     def w_home(i):
         return dp, 2 * (w_first + 4 * i) + w_axis
 
+    def w_part(pair, at):
+        return w_all.at[pair, pl.ds(pl.multiple_of(at * quarter, quarter), quarter)]
+
     def w_ends(k):
         src = w.at[pl.ds(pl.multiple_of(w_other * quarter, quarter), quarter), pl.ds(k * two_kv, two_kv)]
-        return src, w_all.at[2 * core + k, w_other]
+        return src, w_part(2 * core + k, w_other)
 
     def w_copy(k, i):
         src, dst = w_ends(k)
@@ -232,11 +235,11 @@
                 w_copy(k, i).start()
 
     def share_w(pair):
-        landed(w_all.at[pair, other], w_recv.at[pair])
+        landed(w_part(pair, other), w_recv.at[pair])
         for d in range(1, 4):
             target = (line_dp(1 - core, lax.rem(other + d, 4), y, x), 2 * z + core)
             moves.remote(
-                w_all.at[pair, other], w_all.at[pair, other], w_send2.at[pair, d], w_recv2.at[pair, d], target
+                w_part(pair, other), w_part(pair, other), w_send2.at[pair, d], w_recv2.at[pair, d], target
             )
 
     def send_latent(d, e):
@@ -303,6 +306,16 @@
     p_t[...] = jnp.zeros_like(p_t)
     ds_t[...] = jnp.zeros_like(ds_t)
 
+    token = z * block + lax.broadcasted_iota(jnp.int32, (1, block), 1)
+    for slot in range(4):
+        pack = pick(core, 4 * y + slot, 4 * slot + x)
+        end = jnp.int32(0)
+        begun = jnp.zeros((1, block), jnp.int32)
+        for k in range(lengths.shape[1]):
+            end = end + lengths[pack, k]
+            begun = jnp.where(token >= end, end, begun)
+        lo[slot] = begun - (z - 1) * block
+
     def order(s):
         return s + (s // 2) * (1 - 2 * lax.rem(s, 2))
 
@@ -331,8 +344,14 @@
                 else:
                     gq_copy(i, there, e, dm, half).start()
 
+    def ahead(d):
+        return 4 * lax.rem(y + d // 4, 4) + lax.rem(x + d % 4, 4)
+
+    def behind(d):
+        return 4 * wrap(y - d // 4, 4) + wrap(x - d % 4, 4)
+
     def r_copy(i, d):
-        there = lax.rem(dp + d, 16)
+        there = ahead(d)
         return pltpu.make_async_remote_copy(
             src_ref=chosen.at[i, there], dst_ref=come.at[i, dp], send_sem=r_send.at[i, d], recv_sem=r_recv.at[i, d],
             device_id=(there, ctx), device_id_type=MESH,
@@ -342,10 +361,11 @@
         for k in range(8):
             landed(relay.at[i, core, pl.ds(4 * other, 4)], gq_recv.at[k, i])
         relay_now[...] = relay[i]
-        for d in (10, 2, 8, 6, 14, 9, 11, 1, 3, 4, 12, 5, 15, 7, 13, 0):
-            there = lax.rem(dp + d, 16)
-            chosen[i, there, 0] = relay_now[0, from_x[there]]
-            chosen[i, there, 1] = relay_now[1, from_y[there]]
+        for d in (10, 2, 8, 1, 3, 4, 12, 5, 15, 7, 13, 6, 14, 9, 11, 0):
+            there = ahead(d)
+            pack = matching[there]
+            chosen[i, there, 0] = relay_now[0, pack]
+            chosen[i, there, 1] = relay_now[1, 4 * lax.rem(pack, 4) + pack // 4]
             if d == 0:
                 pltpu.make_async_copy(chosen.at[i, there], come.at[i, dp], r_recv.at[i, d]).start()
             else:
@@ -359,7 +379,7 @@
         )
 
     def weight_first(i):
-        dw[i] = dw_acc[...].astype(BF).reshape(4, quarter, two_kv)
+        dw[i] = dw_acc[lax.rem(i, 2)].astype(BF).reshape(4, quarter, two_kv)
         for d in (2, 1, 3, 0):
             if d == 0:
                 pltpu.make_async_copy(dw.at[i, other], dw_parts.at[i, other], dw_recv.at[i, d]).start()
@@ -442,16 +462,21 @@
             d_copy(s, slot).start()
 
     def step(n, _):
-        i, s = n // 4, lax.rem(n, 4)
+        early = jnp.where(n < 8, 1, 0)
+        i = early * lax.rem(n, 2) + (1 - early) * (n // 4)
+        s = early * (n // 2) + (1 - early) * lax.rem(n, 4)
         pair = pair_of(i)
         d = order(s)
         slot = slot_of(s)
 
         @pl.when(s == 0)
         def _():
-            dw_acc[...] = jnp.zeros_like(dw_acc)
+            dw_acc[lax.rem(i, 2)] = jnp.zeros(dw_acc.shape[1:], F32)
+
+        @pl.when(s == 0)
+        def _():
             for dm in range(1, 4):
-                landed(w_all.at[pair, wrap(other - dm, 4)], w_recv2.at[pair, dm])
+                landed(w_part(pair, wrap(other - dm, 4)), w_recv2.at[pair, dm])
 
         @pl.when(i == 0)
         def _():
@@ -461,7 +486,7 @@
             half = lax.rem(core + e, 2)
             landed(q_all.at[pair, slot, half], recv.at[0, pair, 4 * e + d])
             landed(g_all.at[pair, slot, half], recv.at[1, pair, 4 * e + d])
-        heads(slot, pair, lo, q_all, g_all, lat_all, w_all, gq, d_acc, dw_acc, p_t, ds_t)
+        heads(slot, pair, lo, q_all, g_all, lat_all, w_all, gq, d_acc, dw_acc.at[lax.rem(i, 2)], p_t, ds_t)
 
         @pl.when(i == 3)
         def _():
@@ -477,14 +502,15 @@
             relay_pair(i)
             weight_first(i)
 
-        @pl.when((s == 2) & (i > 0))
-        def _():
-            deliver(i - 1)
-            weight_second(i - 1)
-
-        @pl.when((s == 2) & (i > 1))
-        def _():
-            weight_third(i - 2)
+        @pl.when((n == 9) | (n == 10) | (n == 14))
+        def _():
+            done = jnp.where(n == 14, 2, n - 9)
+            deliver(done)
+            weight_second(done)
+
+        @pl.when((n == 12) | (n == 13))
+        def _():
+            weight_third(n - 12)
 
         return 0
 
@@ -509,7 +535,7 @@
     landed(d_cross, c_recv)
     d_sum[core] += d_cross[...]
     for d in range(16):
-        there = lax.rem(dp + d, 16)
+        there = ahead(d)
         if d == 0:
             moves.local(d_sum.at[core, there], d_relay.at[dp], a_recv.at[d])
         else:
@@ -517,7 +543,7 @@
 
     def put(i):
         for d in range(15, -1, -1):
-            source = wrap(dp - d, 16)
+            source = behind(d)
             landed(come.at[i, source], r_recv.at[i, d])
             sy, sx = source // 4, lax.rem(source, 4)
             for j, at, row in ((0, 8 * block_at(sx, z), sy), (1, 8 * block_at(sy, z) + 4, sx)):
@@ -535,8 +561,8 @@
     for d in range(16):
         landed(d_relay.at[dp], a_recv.at[d])
     for d in range(16):
-        there = lax.rem(dp + d, 16)
-        d_pick[there] = d_relay[from_x[there]]
+        there = ahead(d)
+        d_pick[there] = d_relay[matching[there]]
         if d == 0:
             moves.local(d_pick.at[there], grad_lat.at[dp], b_recv.at[d])
         else:
@@ -584,13 +610,12 @@
     landed(grad_q, out_sem)
 
 
-def main_part(lo, from_x, from_y, q, latent, w, g):
+def main_part(lengths, matching, q, latent, w, g):
     rows = q.shape[0]
     block, window = 2 * rows, 4 * rows
     quarter = LATENT // 4
     two_q, two_v, two_kv = 2 * QK, 2 * VDIM, 2 * KV
     dma = pltpu.SemaphoreType.DMA
-    vmem = pl.BlockSpec(memory_space=pltpu.VMEM)
     smem = pl.BlockSpec(memory_space=pltpu.SMEM)
     return pl.pallas_call(
         main_kernel,
@@ -599,13 +624,14 @@
             jax.ShapeDtypeStruct((16, rows // 16, WIDE), F32),
             jax.ShapeDtypeStruct((2, 2, quarter // 8, two_kv), F32),
         ],
-        in_specs=[vmem, smem, smem] + [ANY] * 4,
+        in_specs=[smem, smem] + [ANY] * 4,
         out_specs=[ANY] * 3,
         scratch_shapes=[
+            pltpu.VMEM((4, 1, block), jnp.int32),
             pltpu.VMEM((4, 4, 2, rows, two_q), BF),
             pltpu.VMEM((4, 4, 2, rows, two_v), BF),
             pltpu.VMEM((4, 4, rows, WIDE), BF),
-            pltpu.VMEM((4, 4, quarter, two_kv), BF),
+            pltpu.VMEM((4, LATENT, two_kv), BF),
             pltpu.VMEM((4, 4, 2, rows, two_q), BF),
             pltpu.VMEM((4, 2, 16, rows // 4, two_q), BF),
             pltpu.VMEM((2, 16, rows // 4, two_q), BF),
@@ -625,7 +651,7 @@
             pltpu.VMEM((4, 8, quarter // 8, two_kv), BF),
             pltpu.VMEM((4, 8, quarter // 8, two_kv), BF),
             pltpu.VMEM((4, quarter // 8, two_kv), F32),
-            pltpu.VMEM((LATENT, two_kv), F32),
+            pltpu.VMEM((2, LATENT, two_kv), F32),
             pltpu.VMEM((2, window, block), BF),
             pltpu.VMEM((2, window, block), BF),
             dma((2, 4, 8)), dma((2, 4, 8)), dma((8,)), dma((8,)), dma((2, 2)), dma((4,)), dma((4, 4)), dma((4, 4)),
@@ -637,24 +663,14 @@
             collective_id=0, has_side_effects=True, vmem_limit_bytes=60 * 1024 * 1024
         ),
         name="heads_and_exchanges",
-    )(lo, from_x, from_y, q, latent, w, g)
+    )(lengths, matching, q, latent, w, g)
 
 
 def body(queries, latent, w_kv, grad_out, doc_lengths, matching):
-    y, x, z, core = place()
-    dp = 4 * y + x
     rows = queries.shape[0]
-    block = 2 * rows
-
-    packs = pick(core, 4 * y + jnp.arange(4), 4 * jnp.arange(4) + x)
-    ends = jnp.cumsum(doc_lengths[packs], axis=1)
-    token = z * block + jnp.arange(block, dtype=jnp.int32)
-    begun = jnp.where(ends[:, None, :] <= token[None, :, None], ends[:, None, :], 0)
-    lo = (jnp.max(begun, axis=2) - (z - 1) * block)[:, None, :].astype(jnp.int32)
-
-    turned = 4 * lax.rem(matching, 4) + matching // 4
-    grad_queries, grad_latent, grad_weight = main_part(lo, matching, turned, queries, latent, w_kv, grad_out)
-    return grad_queries, grad_latent.reshape(rows, WIDE), grad_weight.transpose(0, 2, 1, 3).reshape(LATENT // 16, -1)
+    grad_queries, grad_latent, grad_weight = main_part(doc_lengths, matching, queries, latent, w_kv, grad_out)
+    grad_weight = grad_weight.transpose(0, 2, 1, 3).reshape(LATENT // 16, -1)
+    return grad_queries, grad_latent.reshape(rows, WIDE), grad_weight
 
 
 def solution(mesh):

time: 186 us -> 175 us (0.941)
  the two profiles are of different devices: /device:TPU:33 before, /device:TPU:1 now
where the time goes in v5:
time: 175 us
  Pallas kernels  165 us (94%)
  local copies, waits for them, and re-layouts  9.07 us (5%)
    pallas_call x1, Pallas kernels, main_part(): pl.pallas_call(main_kernel, out_shape=[jax.ShapeDtypeStruct(q.shape, BF),...  165 us
    unnamed x4, local copies, waits for them, and re-layouts  8.06 us

profile of v5, /device:TPU:1, one launch (start us, length us, event | category | flops | bytes accessed | tf_op | source)
XLA Modules:
  0.0 174.6 jit_solution(10465110086745531131)
XLA Ops:
  0.6 1.7 copy.11.latent
  2.3 164.9 %heads_and_exchanges.1 = (bf16[128,12288]{1,0:T(8,128)(2,1)}, f32[16,8,576]{2,1,0:T(8,128)}, f32[2,2,16,512]{3,2,1,0:T(8,128)}) custom-call(s32[16,16]{1,0:T(8,128)} %lengths.1, s32[16]{0:T(128)} %matching.1, bf16[128,12288]{1,0:T(8,128)(2,1)} %q.1, bf16[128,576]{1,0:T(8,128)(2,1)} %copy.11.latent, bf16[512,1024]{1,0:T(8,128)(2,1)} %w.1, bf16[128,8192]{1,0:T(8,128)(2,1)} %g.1), custom_call_target="tpu_custom_call" | custom-call | tf_op jit(solution)/shard_map/heads_and_exchanges/pallas_call | solution.py:620
  167.3 1.8 %copy.13 = f32[128,576]{0,1:T(8,128)} copy(f32[128,576]{1,0:T(8,128)} %bitcast.6) | data formatting | bytes 589824
  169.1 1.0 copy.12
  170.1 0.7 copy.14
  170.8 3.8 %copy.16 = bf16[128,12288]{1,0:T(8,128)(2,1)} copy(bf16[128,12288]{1,0:T(8,128)(2,1)} %get-tuple-element.18) | data formatting | bytes 6291456

commit v6 on v5

--- a/solution.py
+++ b/solution.py
@@ -253,22 +253,32 @@
             target = (line_dp(axis, lax.rem(spot + d, 4), y, x), 2 * z + axis)
             moves.remote(latent, dst, l_send.at[k], l_recv.at[k], target)
 
-    def send_rows(pair, d, e):
+    def rows_ends(kind, pair, d, e):
         axis = lax.rem(core + e, 2)
         spot = pick(axis, x, y)
         there = lax.rem(spot + d, 4)
         target = (line_dp(axis, there, y, x), 2 * z + axis)
-        k = 4 * e + d
         at = 4 * (2 * block_at(there, z) + axis) + pair
-        q_part = q.at[:, pl.ds(pl.multiple_of(at * two_q, two_q), two_q)]
-        g_part = g.at[:, pl.ds(pl.multiple_of(at * two_v, two_v), two_v)]
-        q_dst, g_dst = q_all.at[pair, spot, core], g_all.at[pair, spot, core]
-        if d == 0 and e == 0:
-            moves.local(q_part, q_dst, recv.at[0, pair, k])
-            moves.local(g_part, g_dst, recv.at[1, pair, k])
-        else:
-            moves.remote(q_part, q_dst, send.at[0, pair, k], recv.at[0, pair, k], target)
-            moves.remote(g_part, g_dst, send.at[1, pair, k], recv.at[1, pair, k], target)
+        src, width, dst = ((q, two_q, q_all), (g, two_v, g_all))[kind]
+        cols = pl.ds(pl.multiple_of(at * width, width), width)
+        return src.at[:, cols], dst.at[pair, spot, core], recv.at[kind, pair, 4 * e + d], target
+
+    def rows_copy(kind, pair, d, e):
+        src, dst, sem, target = rows_ends(kind, pair, d, e)
+        return pltpu.make_async_remote_copy(
+            src_ref=src, dst_ref=dst, send_sem=send.at[kind, pair, 4 * e + d], recv_sem=sem,
+            device_id=target, device_id_type=MESH,
+        )
+
+    def send_rows(pair):
+        for d in (0, 1, 3, 2):
+            for e in range(2):
+                for kind in range(2):
+                    if d == 0 and e == 0:
+                        src, dst, sem, _ = rows_ends(kind, pair, d, e)
+                        pltpu.make_async_copy(src, dst, sem).start()
+                    else:
+                        rows_copy(kind, pair, d, e).start()
 
     def forward_latent(d):
         slot = wrap(mine - d, 4)
@@ -284,9 +294,7 @@
         for e in range(2):
             send_latent(d, e)
     send_w(1)
-    for d in (0, 1, 3, 2):
-        for e in range(2):
-            send_rows(0, d, e)
+    send_rows(0)
     d_acc[...] = jnp.zeros_like(d_acc)
     forward_latent(0)
     share_w(0)
@@ -294,15 +302,9 @@
     share_w(2)
     forward_latent(3)
     forward_latent(2)
-    for d in (0, 1, 3, 2):
-        for e in range(2):
-            send_rows(2, d, e)
+    send_rows(2)
     share_w(1)
     share_w(3)
-    for pair in (1, 3):
-        for d in (0, 1, 3, 2):
-            for e in range(2):
-                send_rows(pair, d, e)
     p_t[...] = jnp.zeros_like(p_t)
     ds_t[...] = jnp.zeros_like(ds_t)
 
@@ -488,6 +490,11 @@
             landed(g_all.at[pair, slot, half], recv.at[1, pair, 4 * e + d])
         heads(slot, pair, lo, q_all, g_all, lat_all, w_all, gq, d_acc, dw_acc.at[lax.rem(i, 2)], p_t, ds_t)
 
+        for turn, waiting in ((0, 1), (3, 3)):
+            @pl.when(n == turn)
+            def _():
+                send_rows(waiting)
+
         @pl.when(i == 3)
         def _():
             d_halo[slot] = d_acc[slot, :block].astype(BF)
@@ -502,15 +509,16 @@
             relay_pair(i)
             weight_first(i)
 
-        @pl.when((n == 9) | (n == 10) | (n == 14))
-        def _():
-            done = jnp.where(n == 14, 2, n - 9)
-            deliver(done)
-            weight_second(done)
-
-        @pl.when((n == 12) | (n == 13))
-        def _():
-            weight_third(n - 12)
+        for done, turn in enumerate((11, 13, 15)):
+            @pl.when(n == turn)
+            def _():
+                deliver(jnp.int32(done))
+                weight_second(jnp.int32(done))
+
+        for done, turn in enumerate((14, 15)):
+            @pl.when(n == turn)
+            def _():
+                weight_third(jnp.int32(done))
 
         return 0
 
@@ -518,8 +526,6 @@
 
     three = jnp.int32(3)
     add_halo(three)
-    deliver(three)
-    weight_second(three)
 
     def collect(s, _):
         landed(d_lat.at[lax.rem(mine + order(s), 4)], d_recv.at[s])
@@ -531,7 +537,6 @@
         total += d_lat[i].astype(F32)
     d_sum[...] = total.reshape(d_sum.shape)
     moves.remote(d_sum.at[1 - core], d_cross, c_send, c_recv, (dp, 2 * z + 1 - core))
-    weight_third(jnp.int32(2))
     landed(d_cross, c_recv)
     d_sum[core] += d_cross[...]
     for d in range(16):
@@ -540,6 +545,8 @@
             moves.local(d_sum.at[core, there], d_relay.at[dp], a_recv.at[d])
         else:
             moves.remote(d_sum.at[core, there], d_relay.at[dp], a_send.at[d], a_recv.at[d], (there, ctx))
+    deliver(three)
+    weight_second(three)
 
     def put(i):
         for d in range(15, -1, -1):
@@ -557,7 +564,6 @@
         put(i)
         return 0
 
-    lax.fori_loop(0, 3, put_early, 0)
     for d in range(16):
         landed(d_relay.at[dp], a_recv.at[d])
     for d in range(16):
@@ -567,6 +573,8 @@
             moves.local(d_pick.at[there], grad_lat.at[dp], b_recv.at[d])
         else:
             moves.remote(d_pick.at[there], grad_lat.at[dp], b_send.at[d], b_recv.at[d], (there, ctx))
+    weight_third(jnp.int32(2))
+    lax.fori_loop(0, 3, put_early, 0)
     weight_third(three)
     put(three)
 
@@ -582,6 +590,16 @@
 
     for copy in moves.sent:
         copy.wait_send()
+
+    def rows_left(pair, _):
+        for d in range(4):
+            for e in range(2):
+                if d or e:
+                    for kind in range(2):
+                        rows_copy(kind, pair, d, e).wait_send()
+        return 0
+
+    lax.fori_loop(0, 4, rows_left, 0)
 
     def close(i, _):
         for k in range(1, 8):

time: 175 us -> 164 us (0.937)
  Pallas kernels: 165 us -> 153 us
    pallas_call x1, Pallas kernels: 165 us -> 153 us  [main_part(): pl.pallas_call(main_kernel, out_shape=[jax.ShapeDtypeStruct(q.shape, BF),...]
where the time goes in v6:
time: 164 us; the launch traced here: 163 us
  Pallas kernels  153 us (93%)
  local copies, waits for them, and re-layouts  9.07 us (6%)
    pallas_call x1, Pallas kernels, main_part(): pl.pallas_call(main_kernel, out_shape=[jax.ShapeDtypeStruct(q.shape, BF),...  153 us
    unnamed x4, local copies, waits for them, and re-layouts  8.06 us

profile of v6, /device:TPU:1, one launch (start us, length us, event | category | flops | bytes accessed | tf_op | source)
XLA Modules:
  0.0 162.7 jit_solution(13867934029714377606)
XLA Ops:
  0.6 1.7 %copy.11.latent = bf16[128,576]{1,0:T(8,128)(2,1)} copy(bf16[128,576]{0,1:T(8,128)(2,1)} %param.7) | data formatting | bytes 294912 | tf_op args[1]
  2.3 153.0 %heads_and_exchanges.1 = (bf16[128,12288]{1,0:T(8,128)(2,1)}, f32[16,8,576]{2,1,0:T(8,128)}, f32[2,2,16,512]{3,2,1,0:T(8,128)}) custom-call(s32[16,16]{1,0:T(8,128)} %lengths.1, s32[16]{0:T(128)} %matching.1, bf16[128,12288]{1,0:T(8,128)(2,1)} %q.1, bf16[128,576]{1,0:T(8,128)(2,1)} %copy.11.latent, bf16[512,1024]{1,0:T(8,128)(2,1)} %w.1, bf16[128,8192]{1,0:T(8,128)(2,1)} %g.1), custom_call_target="tpu_custom_call" | custom-call | tf_op jit(solution)/shard_map/heads_and_exchanges/pallas_call | solution.py:638
  155.4 1.8 %copy.13 = f32[128,576]{0,1:T(8,128)} copy(f32[128,576]{1,0:T(8,128)} %bitcast.6) | data formatting | bytes 589824
  157.2 1.0 copy.12
  158.2 0.7 copy.14
  158.9 3.8 %copy.16 = bf16[128,12288]{1,0:T(8,128)(2,1)} copy(bf16[128,12288]{1,0:T(8,128)(2,1)} %get-tuple-element.18) | data formatting | bytes 6291456

commit v7 on v6

--- a/solution.py
+++ b/solution.py
@@ -506,8 +506,8 @@
 
         @pl.when(s == 3)
         def _():
+            weight_first(i)
             relay_pair(i)
-            weight_first(i)
 
         for done, turn in enumerate((11, 13, 15)):
             @pl.when(n == turn)
@@ -545,8 +545,8 @@
             moves.local(d_sum.at[core, there], d_relay.at[dp], a_recv.at[d])
         else:
             moves.remote(d_sum.at[core, there], d_relay.at[dp], a_send.at[d], a_recv.at[d], (there, ctx))
+    weight_second(three)
     deliver(three)
-    weight_second(three)
 
     def put(i):
         for d in range(15, -1, -1):

time: 164 us -> 163 us (level)
  no operation moved by 1% of the time
where the time goes in v7:
time: 163 us
  Pallas kernels  153 us (94%)
  local copies, waits for them, and re-layouts  9.07 us (6%)
    pallas_call x1, Pallas kernels, main_part(): pl.pallas_call(main_kernel, out_shape=[jax.ShapeDtypeStruct(q.shape, BF),...  153 us
    unnamed x4, local copies, waits for them, and re-layouts  8.06 us

profile of v7, /device:TPU:1, one launch (start us, length us, event | category | flops | bytes accessed | tf_op | source)
XLA Modules:
  0.0 162.9 jit_solution(10728215998576911362)
XLA Ops:
  0.6 1.7 %copy.11.latent = bf16[128,576]{1,0:T(8,128)(2,1)} copy(bf16[128,576]{0,1:T(8,128)(2,1)} %param.7) | data formatting | bytes 294912 | tf_op args[1]
  2.3 153.2 %heads_and_exchanges.1 = (bf16[128,12288]{1,0:T(8,128)(2,1)}, f32[16,8,576]{2,1,0:T(8,128)}, f32[2,2,16,512]{3,2,1,0:T(8,128)}) custom-call(s32[16,16]{1,0:T(8,128)} %lengths.1, s32[16]{0:T(128)} %matching.1, bf16[128,12288]{1,0:T(8,128)(2,1)} %q.1, bf16[128,576]{1,0:T(8,128)(2,1)} %copy.11.latent, bf16[512,1024]{1,0:T(8,128)(2,1)} %w.1, bf16[128,8192]{1,0:T(8,128)(2,1)} %g.1), custom_call_target="tpu_custom_call" | custom-call | tf_op jit(solution)/shard_map/heads_and_exchanges/pallas_call | solution.py:638
  155.5 1.8 %copy.13 = f32[128,576]{0,1:T(8,128)} copy(f32[128,576]{1,0:T(8,128)} %bitcast.6) | data formatting | bytes 589824
  157.3 1.0 copy.12
  158.4 0.7 copy.14
  159.0 3.8 %copy.16 = bf16[128,12288]{1,0:T(8,128)(2,1)} copy(bf16[128,12288]{1,0:T(8,128)(2,1)} %get-tuple-element.18) | data formatting | bytes 6291456
